TPU v7x, 512 devices: a whole 4x4x16 slice. The times are simulated.
512 devices in a mesh: grp: 8 (over y_lo, x), row: 64 (over z, y_hi, core).
Axes of the slice: x: 4, y: 4 (y_hi: 2, y_lo: 2; y = y_hi * 2 + y_lo), z: 16, core: 2. Of those that a mesh axis runs over, the one named last changes fastest.
Arguments:
- descriptors: bfloat16 [65536, 1024], P('row'), may hold values from -60 to 60
- sparse_points: bfloat16 [4096, 1024], P('grp'), may hold values from -60 to 60
Outputs:
- gram_slab: float32 [4096, 2048], P(('grp', 'row'))
All inputs are finite; a program needn't handle non-finite values.
Results may differ from a plain program's by a relative error of at most 0.0003.
Values may be sent and summed in bfloat16 or wider, within the bound.
No kernel may reach another device: no remote copies, remote signals or barrier semaphores. Data moves between devices by JAX's collectives and lax.ppermute only.
A program may use at most 64 MiB of HBM per device.

v0:
```python
import jax
import jax.numpy as jnp
from jax import lax
from jax.sharding import PartitionSpec as P

ZETA = 4


kernel_variance = 24.0


def passed_along(value, axis, steps):
    count = lax.axis_size(axis)
    pairs = [(source, (source + steps) % count) for source in range(count)]
    return lax.ppermute(value, axis, pairs)


def inverse_norms(values):
    floats = values.astype(jnp.float32)
    return lax.rsqrt(jnp.sum(floats * floats, axis=1) + 1e-06)


def kernel_block(left, left_inv, right):
    inner = lax.dot_general(
        left, right, (((1,), (1,)), ((), ())), preferred_element_type=jnp.float32
    )
    cosine = inner * left_inv[:, None] * inverse_norms(right)[None, :]
    return (kernel_variance * cosine**ZETA).astype(jnp.bfloat16)


def shards(descriptors, sparse_points):
    rows_local = descriptors.shape[0]
    groups = lax.axis_size("grp")
    band = min(4, groups)
    envs = rows_local * lax.axis_size("row")
    env_inv = inverse_norms(descriptors)
    own = kernel_block(descriptors, env_inv, sparse_points)
    columns = [own]
    for offset in range(1, band):
        columns.append(passed_along(own, "grp", -offset))
    joined = jnp.concatenate(columns, axis=1)
    summed = lax.psum_scatter(
        lax.dot_general(own, joined, (((0,), (0,)), ((), ())), preferred_element_type=jnp.float32),
        "row",
        scatter_dimension=0,
        tiled=True,
    )
    return summed / envs


def solution(mesh):
    return jax.shard_map(
        shards,
        mesh=mesh,
        in_specs=(P("row", None), P("grp", None)),
        out_specs=P(("grp", "row"), None),
        check_vma=False,
    )
```

profile of v0, /device:TPU:2, one launch (start us, length us, event | category | flops | bytes accessed | tf_op | source)
XLA Modules:
  0.0 333.7 jit_solution(17297137288213934354)
XLA Ops:
  6.5 0.0 reduce-scatter.2.cloned.1.call-start
  6.5 1.5 multiply_reduce_fusion.1
  8.0 2.1 multiply_reduce_fusion
  10.1 3.3 multiply_convert_fusion
  13.4 4.4 %collective-permute-start.2 = (bf16[1024,512]{0,1:T(8,128)(2,1)S(1)}, bf16[1024,512]{0,1:T(8,128)(2,1)S(1)}, u32[]{:S(2)}, u32[]{:S(2)}) collective-permute-start(bf16[1024,512]{0,1:T(8,128)(2,1)S(1)} %multiply_convert_fusion), channel_id=1, source_target_pairs={{0,320},{64,384},{128,448},{192,0},{256,64},{320,128},{384,192},{4... | collective-permute-start | bytes 3145736 | tf_op jit(solution)/shard_map/ppermute | solution.py:15
  17.8 3.0 collective-permute-start.1
  20.9 4.2 %collective-permute-start = (bf16[1024,512]{0,1:T(8,128)(2,1)S(1)}, bf16[1024,512]{0,1:T(8,128)(2,1)S(1)}, u32[]{:S(2)}, u32[]{:S(2)}) collective-permute-start(bf16[1024,512]{0,1:T(8,128)(2,1)S(1)} %multiply_convert_fusion), channel_id=1, source_target_pairs={{0,448},{64,0},{128,64},{192,128},{256,192},{320,256},{384,320},{4... | collective-permute-start | bytes 3145736 | tf_op jit(solution)/shard_map/ppermute | solution.py:15
  25.1 19.1 %collective-permute-done.2 = bf16[1024,512]{0,1:T(8,128)(2,1)S(1)} collective-permute-done((bf16[1024,512]{0,1:T(8,128)(2,1)S(1)}, bf16[1024,512]{0,1:T(8,128)(2,1)S(1)}, u32[]{:S(2)}, u32[]{:S(2)}) %collective-permute-start.2) | collective-permute-done | bytes 1048608 | tf_op jit(solution)/shard_map/ppermute | solution.py:15
  44.2 11.4 %collective-permute-done.1 = bf16[1024,512]{0,1:T(8,128)(2,1)S(1)} collective-permute-done((bf16[1024,512]{0,1:T(8,128)(2,1)S(1)}, bf16[1024,512]{0,1:T(8,128)(2,1)S(1)}, u32[]{:S(2)}, u32[]{:S(2)}) %collective-permute-start.1) | collective-permute-done | bytes 1048608 | tf_op jit(solution)/shard_map/ppermute | solution.py:15
  55.5 21.0 %collective-permute-done = bf16[1024,512]{0,1:T(8,128)(2,1)S(1)} collective-permute-done((bf16[1024,512]{0,1:T(8,128)(2,1)S(1)}, bf16[1024,512]{0,1:T(8,128)(2,1)S(1)}, u32[]{:S(2)}, u32[]{:S(2)}) %collective-permute-start) | collective-permute-done | bytes 1048608 | tf_op jit(solution)/shard_map/ppermute | solution.py:15
  76.5 8.0 %fusion = f32[512,2048]{1,0:T(8,128)} fusion(bf16[1024,512]{0,1:T(8,128)(2,1)S(1)} %multiply_convert_fusion, bf16[1024,512]{0,1:T(8,128)(2,1)S(1)} %collective-permute-done.2, bf16[1024,512]{0,1:T(8,128)(2,1)S(1)} %collective-permute-done.1, bf16[1024,512]{0,1:T(8,128)(2,1)S(1)} %collective-permute-done), kind=kOutput, calls=%fused_computation | convolution fusion | flops 2164260864 | bytes 8388608 | tf_op jit(solution)/shard_map/dot_general | solution.py:43
  84.5 0.0 reduce-scatter.2.cloned.1.call-update
  84.6 240.8 %reduce-scatter.2.cloned.1.call-done = f32[8,2048]{1,0:T(8,128)} async-done(((f32[512,2048]{1,0:T(8,128)}), f32[8,2048]{1,0:T(8,128)}) %reduce-scatter.2.cloned.1.call-update) | async-done | bytes 65552 | tf_op jit(solution)/shard_map/reduce_scatter | solution.py:42
  325.3 1.5 broadcast_multiply_fusion
  (2 shorter events, 0.0 us)
Async XLA Ops:
  6.5 318.8 %reduce-scatter.2.cloned.1.call-start = ((), (), s32[]{:S(2)}) async-start(), calls=%async_computation.1 | async-start | bytes 4259840 | tf_op jit(solution)/shard_map/reduce_scatter | solution.py:42
  13.4 30.8 %collective-permute-start.2 = (bf16[1024,512]{0,1:T(8,128)(2,1)S(1)}, bf16[1024,512]{0,1:T(8,128)(2,1)S(1)}, u32[]{:S(2)}, u32[]{:S(2)}) collective-permute-start(bf16[1024,512]{0,1:T(8,128)(2,1)S(1)} %multiply_convert_fusion), channel_id=1, source_target_pairs={{0,320},{64,384},{128,448},{192,0},{256,64},{320,128},{384,192},{4... | collective-permute-start | bytes 3145736 | tf_op jit(solution)/shard_map/ppermute | solution.py:15
  17.8 37.7 %collective-permute-start.1 = (bf16[1024,512]{0,1:T(8,128)(2,1)S(1)}, bf16[1024,512]{0,1:T(8,128)(2,1)S(1)}, u32[]{:S(2)}, u32[]{:S(2)}) collective-permute-start(bf16[1024,512]{0,1:T(8,128)(2,1)S(1)} %multiply_convert_fusion), channel_id=1, source_target_pairs={{0,384},{64,448},{128,0},{192,64},{256,128},{320,192},{384,256},{4... | collective-permute-start | bytes 3145736 | tf_op jit(solution)/shard_map/ppermute | solution.py:15
  20.9 55.7 %collective-permute-start = (bf16[1024,512]{0,1:T(8,128)(2,1)S(1)}, bf16[1024,512]{0,1:T(8,128)(2,1)S(1)}, u32[]{:S(2)}, u32[]{:S(2)}) collective-permute-start(bf16[1024,512]{0,1:T(8,128)(2,1)S(1)} %multiply_convert_fusion), channel_id=1, source_target_pairs={{0,448},{64,0},{128,64},{192,128},{256,192},{320,256},{384,320},{4... | collective-permute-start | bytes 3145736 | tf_op jit(solution)/shard_map/ppermute | solution.py:15
Sparse Core Ops, SparseCore 0:
  84.7 240.6 reduce-scatter.1
where the time goes:
time: 334 us
  waiting for transfers between devices  292 us (87%)
  between operations  13.4 us (4%)
  starting transfers between devices  11.7 us (4%)
  matrix products  11.3 us (3%)
  other arithmetic  5.06 us (2%)
    reduce_scatter x1, waiting for transfers between devices, shards(): lax.psum_scatter(lax.dot_general(own, joined, (((0,), (0,)), ((), ())), p...  241 us
    ppermute x3, waiting for transfers between devices, passed_along(): return lax.ppermute(value, axis, pairs)  51.4 us
    ppermute x3, starting transfers between devices, passed_along(): return lax.ppermute(value, axis, pairs)  11.7 us
    dot_general x1, matrix products, shards(): lax.dot_general(own, joined, (((0,), (0,)), ((), ())), preferred_element_...  8 us
  transfers between devices with their start and end apart: 4, of which 4 were waited for; matrix products, arithmetic and copies ran while one was open for 0% of the time, Pallas kernels for 0%

commit v1 on v0

v1 whole, which is shorter than its diff:
```python
import functools

import jax
import jax.numpy as jnp
from jax import lax
from jax.experimental import pallas as pl
from jax.experimental.pallas import tpu as pltpu
from jax.sharding import Mesh
from jax.sharding import PartitionSpec as P

NAMES = ("y_lo", "x", "z_hi", "z_lo", "y_hi", "core")
SIZES = (2, 4, 8, 2, 2, 2)
KERNEL_VARIANCE = 24.0
D = 1024
ENV = 1024
BLK = 512
HALF = BLK // 2
WIDE = 4 * HALF
TARGET = 14
VMEM = 60 * 1024 * 1024


def flat(y_lo, x, z_hi, z_lo, y_hi, core):
    return ((((y_lo * 4 + x) * 8 + z_hi) * 2 + z_lo) * 2 + y_hi) * 2 + core


def from_group(steps):
    pairs = []
    for y_lo in range(2):
        for x in range(4):
            source = (y_lo * 4 + x + steps) % 8
            s_lo, s_x = divmod(source, 4)
            for z_hi in range(8):
                for z_lo in range(2):
                    for y_hi in range(2):
                        for core in range(2):
                            y = y_hi * 2 + y_lo
                            if s_lo != y_lo:
                                y = (y + (1 if core == 0 else -1)) % 4
                            pairs.append((flat(s_lo, s_x, z_hi, z_lo, y // 2, core), flat(y_lo, x, z_hi, z_lo, y_hi, core)))
    return pairs


def whole(*shape):
    return pl.BlockSpec(memory_space=pltpu.VMEM)


def call(body, outs, inputs, scratch=(), flops=0):
    size = sum(v.size * v.dtype.itemsize for v in inputs)
    return pl.pallas_call(
        body,
        out_shape=outs,
        in_specs=[pl.BlockSpec(memory_space=pltpu.VMEM)] * len(inputs),
        out_specs=jax.tree.map(lambda _: pl.BlockSpec(memory_space=pltpu.VMEM), outs),
        scratch_shapes=list(scratch),
        compiler_params=pltpu.CompilerParams(vmem_limit_bytes=VMEM),
        cost_estimate=pl.CostEstimate(flops=flops, bytes_accessed=size, transcendentals=0),
    )(*inputs)


def nt(left, right):
    return lax.dot_general(left, right, (((1,), (1,)), ((), ())), preferred_element_type=jnp.float32)


def point_inverse(points):
    floats = points.astype(jnp.float32)
    return lax.rsqrt(jnp.sum(floats * floats, axis=1, keepdims=True) + 1e-06)


def powered(inner, left_inv, right_inv):
    cosine = inner * left_inv * right_inv
    square = cosine * cosine
    return (KERNEL_VARIANCE * (square * square)).astype(jnp.bfloat16)


def own_kernel(points, rows, rows_inv, out):
    inv = point_inverse(points[...])

    @pl.loop(0, ENV // 256)
    def _(i):
        part = pl.ds(pl.multiple_of(i * 256, 256), 256)
        out[:, part] = powered(nt(points[...], rows[part, :]), inv, rows_inv[:, part])


def exponent(largest):
    return jnp.floor(jnp.log2(jnp.maximum(largest, 1e-37)))


def coded(values, e, rows, width):
    half = jnp.exp2(0.5 * (TARGET - e))
    scaled = values * half * half
    scaled = scaled * scaled
    scaled = scaled * scaled
    scaled = scaled * scaled
    row = lax.broadcasted_iota(jnp.int32, values.shape, 0)
    lane = lax.broadcasted_iota(jnp.int32, values.shape, 1)
    number = jnp.broadcast_to(e.astype(jnp.int32) + 128, values.shape)
    bit = lax.shift_right_logical(number, jnp.minimum(lane, 30)) & 1
    marked = (row % rows == 0) & (lane < 8)
    scaled = jnp.where(marked, jnp.maximum(scaled, 1e-35), scaled)
    return jnp.where(marked & (bit == 1), -scaled, scaled).astype(jnp.bfloat16)


def decoded(chunk):
    floats = chunk.astype(jnp.float32)
    head = floats[0:1, 0:128]
    lane = lax.broadcasted_iota(jnp.int32, head.shape, 1)
    weight = jnp.left_shift(1, jnp.minimum(lane, 7)).astype(jnp.float32)
    number = jnp.sum(jnp.where((lane < 8) & (head < 0), weight, 0.0), axis=1, keepdims=True)
    return jnp.exp2(jnp.log2(jnp.abs(floats)) * 0.125 + (number - (128 + TARGET)))


def gram_kernel(core, a0, a1, d0, d1, e0, e1, b1, b2_low, b2_high, b3, out, points, k0, k1, gram):
    points[0:256, :] = b1[...]
    points[256:384, :] = b2_low[...]
    points[384:512, :] = b2_high[...]
    points[512:768, :] = b3[...]
    inv = point_inverse(points[...])
    mine = pl.ds(pl.multiple_of(core[0] * HALF, HALF), HALF)
    for a, rows, rows_inv, k in ((a0, d0, e0, k0), (a1, d1, e1, k1)):
        k[0:HALF, :] = a[mine, :]

        @pl.loop(0, ENV // 256)
        def _(i):
            part = pl.ds(pl.multiple_of(i * 256, 256), 256)
            k[HALF:, part] = powered(nt(points[...], rows[part, :]), inv, rows_inv[:, part])

    def step(i, largest):
        part = pl.ds(pl.multiple_of(i * 128, 128), 128)
        block = nt(a0[part, :], k0[...]) + nt(a1[part, :], k1[...])
        gram[part, :] = block
        return jnp.maximum(largest, jnp.max(block, axis=(0, 1), keepdims=True))

    e = exponent(lax.fori_loop(0, BLK // 128, step, jnp.zeros((1, 1), jnp.float32)))

    @pl.loop(0, 8)
    def _(z_hi):
        for d in range(4):
            values = gram[pl.ds(pl.multiple_of(z_hi * 64 + d * 16, 16), 16), :]
            out[pl.ds(pl.multiple_of(d * 128 + z_hi * 16, 16), 16), :] = coded(values, e, 16, WIDE)


def middle_kernel(chunks, out):
    total = decoded(chunks[0:128, :])
    for s in range(1, 4):
        total = total + decoded(chunks[s * 128 : (s + 1) * 128, :])
    e = exponent(jnp.max(total, axis=(0, 1), keepdims=True))
    out[...] = coded(total, e, 8, WIDE)


def last_kernel(scale, chunks, out):
    for core in range(2):
        total = jnp.zeros((8, WIDE), jnp.float32)
        for z_hi in range(8):
            total = total + decoded(chunks[z_hi * 2 + core, :, :])
        total = total * scale
        for j in range(4):
            out[:, j * BLK + core * HALF : j * BLK + (core + 1) * HALF] = total[:, j * HALF : (j + 1) * HALF]


def env_inverse(rows):
    floats = rows.astype(jnp.float32)
    return lax.rsqrt(jnp.sum(floats * floats, axis=1) + 1e-06).reshape(1, ENV)


def shards(descriptors, sparse_points):
    f32, bf16 = jnp.float32, jnp.bfloat16
    core = lax.axis_index("core")
    mine = lax.dynamic_slice_in_dim(sparse_points, core * HALF, HALF, 0)
    b1 = lax.ppermute(mine, NAMES, from_group(1))
    b3 = lax.ppermute(mine, NAMES, from_group(3))
    other = lax.ppermute(descriptors, "core", [(0, 1), (1, 0)])
    b2_low = lax.ppermute(b1[: HALF // 2], NAMES, from_group(1))
    b2_high = lax.ppermute(b3[HALF // 2 :], NAMES, from_group(-1))

    columns = []
    for rows in (descriptors, other):
        inv = env_inverse(rows)
        own = call(
            own_kernel, jax.ShapeDtypeStruct((BLK, ENV), bf16), (sparse_points, rows, inv), flops=2 * BLK * ENV * D
        )
        columns.append((own, rows, inv))
    (a0, d0, e0), (a1, d1, e1) = columns

    number = core.astype(jnp.int32).reshape(1)
    inputs = (number, a0, a1, d0, d1, e0, e1, b1, b2_low, b2_high, b3)
    sent = pl.pallas_call(
        gram_kernel,
        out_shape=jax.ShapeDtypeStruct((BLK, WIDE), bf16),
        in_specs=[pl.BlockSpec(memory_space=pltpu.SMEM)] + [pl.BlockSpec(memory_space=pltpu.VMEM)] * 10,
        out_specs=pl.BlockSpec(memory_space=pltpu.VMEM),
        scratch_shapes=[
            pltpu.VMEM((3 * HALF, D), bf16),
            pltpu.VMEM((WIDE, ENV), bf16),
            pltpu.VMEM((WIDE, ENV), bf16),
            pltpu.VMEM((BLK, WIDE), f32),
        ],
        compiler_params=pltpu.CompilerParams(vmem_limit_bytes=VMEM),
        cost_estimate=pl.CostEstimate(flops=10 * 2**30, bytes_accessed=12 * 2**20, transcendentals=0),
    )(*inputs)
    got = lax.all_to_all(sent, ("z_lo", "y_hi"), 0, 0, tiled=True)
    sent = call(middle_kernel, jax.ShapeDtypeStruct((128, WIDE), bf16), (got,))
    got = lax.all_to_all(sent.reshape(16, 8, WIDE), ("z_hi", "core"), 0, 0, tiled=True)
    scale = 1.0 / (ENV * 64)
    return call(functools.partial(last_kernel, scale), jax.ShapeDtypeStruct((8, 4 * BLK), f32), (got,))


def solution(mesh):
    fine = Mesh(mesh.devices.reshape(SIZES), NAMES)
    return jax.shard_map(
        shards,
        mesh=fine,
        in_specs=(P(("z_hi", "z_lo", "y_hi", "core"), None), P(("y_lo", "x"), None)),
        out_specs=P(NAMES, None),
        check_vma=False,
    )
```

time: 334 us -> 116 us (0.35)
  the two profiles are of different devices: /device:TPU:2 before, /device:TPU:1 now
where the time goes in v1:
time: 116 us
  blocking collectives  56.6 us (49%)
  Pallas kernels  31.3 us (27%)
  starting transfers between devices  17 us (15%)
  waiting for transfers between devices  5.1 us (4%)
  other arithmetic  3.91 us (3%)
  local copies, waits for them, and re-layouts  1.91 us (2%)
    all_to_all x1, blocking collectives, shards(): lax.all_to_all(sent.reshape(16, 8, WIDE), ('z_hi', 'core'), 0, 0, tiled=T...  35.5 us
    all_to_all x1, blocking collectives, shards(): got = lax.all_to_all(sent, ('z_lo', 'y_hi'), 0, 0, tiled=True)  21 us
    pallas_call x1, Pallas kernels, shards(): pl.pallas_call(gram_kernel, out_shape=jax.ShapeDtypeStruct((BLK, WIDE), b...  16.5 us
    pallas_call x4, Pallas kernels, call(): pl.pallas_call(body, out_shape=outs, in_specs=[pl.BlockSpec(memory_space=...  14.7 us
    ppermute x1, starting transfers between devices, shards(): other = lax.ppermute(descriptors, 'core', [(0, 1), (1, 0)])  8.78 us
    ppermute x1, waiting for transfers between devices, shards(): b3 = lax.ppermute(mine, NAMES, from_group(3))  5.05 us
    reduce_sum x2, other arithmetic, env_inverse(): return lax.rsqrt(jnp.sum(floats * floats, axis=1) + 1e-06).reshape(1, ENV)  2.55 us
    ppermute x1, starting transfers between devices, shards(): b2_low = lax.ppermute(b1[:HALF // 2], NAMES, from_group(1))  2.47 us
  transfers between devices with their start and end apart: 5, of which 1 were waited for; matrix products, arithmetic and copies ran while one was open for 4% of the time, Pallas kernels for 9%

profile of v1, /device:TPU:1, one launch (start us, length us, event | category | flops | bytes accessed | tf_op | source)
XLA Modules:
  0.0 115.9 jit_solution(719121082519302987)
XLA Ops:
  0.0 8.8 %collective-permute-start = (bf16[1024,1024]{1,0:T(8,128)(2,1)}, bf16[1024,1024]{1,0:T(8,128)(2,1)S(1)}, u32[]{:S(2)}, u32[]{:S(2)}) collective-permute-start(bf16[1024,1024]{1,0:T(8,128)(2,1)} %d0.1), channel_id=1, source_target_pairs={{0,1},{1,0},{2,3},{3,2},{4,5},{5,4},{6,7},{7,6},{8,9},{9,8},{10,11... | collective-permute-start | bytes 6291464 | tf_op jit(solution)/shard_map/ppermute | solution.py:172
  8.8 1.1 constant_dynamic-slice_fusion
  9.9 1.9 %collective-permute-start.3 = (bf16[256,1024]{1,0:T(8,128)(2,1)S(1)}, bf16[256,1024]{1,0:T(8,128)(2,1)S(1)}, u32[]{:S(2)}, u32[]{:S(2)}) collective-permute-start(bf16[256,1024]{1,0:T(8,128)(2,1)S(1)} %constant_dynamic-slice_fusion), channel_id=1, source_target_pairs={{192,0},{193,1},{194,2},{195,3},{196,4},{197,5},{198,6},{199,7},{2... | collective-permute-start | bytes 1572872 | tf_op jit(solution)/shard_map/ppermute | solution.py:171
  11.8 1.9 %collective-permute-start.1 = (bf16[256,1024]{1,0:T(8,128)(2,1)S(1)}, bf16[256,1024]{1,0:T(8,128)(2,1)S(1)}, u32[]{:S(2)}, u32[]{:S(2)}) collective-permute-start(bf16[256,1024]{1,0:T(8,128)(2,1)S(1)} %constant_dynamic-slice_fusion), channel_id=1, source_target_pairs={{64,0},{65,1},{66,2},{67,3},{68,4},{69,5},{70,6},{71,7},{72,8},{73... | collective-permute-start | bytes 1572872 | tf_op jit(solution)/shard_map/ppermute | solution.py:170
  13.7 2.1 %multiply_reduce_fusion.1 = f32[1024]{0:T(1024)S(1)} fusion(bf16[1024,1024]{1,0:T(8,128)(2,1)} %d0.1), kind=kLoop, calls=%fused_computation.1 | loop fusion | flops 3144704 | bytes 2101248 | tf_op jit(solution)/shard_map/reduce_sum | solution.py:163
  15.8 0.6 add_rsqrt_fusion.1
  16.4 5.1 %shard_map.28.a0 = bf16[512,1024]{1,0:T(8,128)(2,1)} custom-call(bf16[512,1024]{1,0:T(8,128)(2,1)} %points.3, bf16[1024,1024]{1,0:T(8,128)(2,1)} %d0.1, f32[1,1024]{1,0:T(1,128)} %bitcast.9), custom_call_target="tpu_custom_call" | custom-call | flops 1073741824 | bytes 3149824 | tf_op jit(solution)/shard_map/pallas_call | solution.py:50
  21.5 5.1 %collective-permute-done.3.b3 = bf16[256,1024]{1,0:T(8,128)(2,1)S(1)} collective-permute-done((bf16[256,1024]{1,0:T(8,128)(2,1)S(1)}, bf16[256,1024]{1,0:T(8,128)(2,1)S(1)}, u32[]{:S(2)}, u32[]{:S(2)}) %collective-permute-start.3) | collective-permute-done | bytes 524320 | tf_op jit(solution)/shard_map/ppermute | solution.py:171
  26.5 0.0 copy-start.1
  26.5 1.9 %collective-permute-start.4 = (bf16[128,1024]{1,0:T(8,128)(2,1)S(1)}, bf16[128,1024]{1,0:T(8,128)(2,1)}, u32[]{:S(2)}, u32[]{:S(2)}) collective-permute-start(bf16[128,1024]{1,0:T(8,128)(2,1)S(1)} %slice.9), channel_id=1, source_target_pairs={{448,0},{451,1},{450,2},{449,3},{452,4},{455,5},{454,6},{453,7},{4... | collective-permute-start | bytes 786440 | tf_op jit(solution)/shard_map/ppermute | solution.py:174
  28.5 0.0 collective-permute-done.1.b1
  28.5 0.0 copy-start.2
  28.5 2.5 %collective-permute-start.2 = (bf16[128,1024]{1,0:T(8,128)(2,1)S(1)}, bf16[128,1024]{1,0:T(8,128)(2,1)S(1)}, u32[]{:S(2)}, u32[]{:S(2)}) collective-permute-start(bf16[128,1024]{1,0:T(8,128)(2,1)S(1)} %slice.8), channel_id=1, source_target_pairs={{64,0},{65,1},{66,2},{67,3},{68,4},{69,5},{70,6},{71,7},{72,8},{73... | collective-permute-start | bytes 786440 | tf_op jit(solution)/shard_map/ppermute | solution.py:173
  31.0 0.0 collective-permute-done.rows.d1
  31.0 0.0 copy-start
  31.0 0.5 multiply_reduce_fusion
  31.5 0.8 add_rsqrt_fusion
  32.3 0.1 copy-done
  32.3 5.1 %shard_map.29.a1 = bf16[512,1024]{1,0:T(8,128)(2,1)} custom-call(bf16[512,1024]{1,0:T(8,128)(2,1)} %points.3, bf16[1024,1024]{1,0:T(8,128)(2,1)} %copy-done, f32[1,1024]{1,0:T(1,128)} %bitcast.11), custom_call_target="tpu_custom_call" | custom-call | flops 1073741824 | bytes 3149824 | tf_op jit(solution)/shard_map/pallas_call | solution.py:50
  37.4 0.0 copy-done.1
  37.4 0.0 copy-done.2
  37.4 0.0 collective-permute-done.4.b2_high
  37.4 0.0 collective-permute-done.2.b2_low
  37.5 0.0 copy-start.3
  37.5 0.7 copy-done.3
  38.2 16.5 %shard_map.30 = bf16[512,1024]{1,0:T(8,128)(2,1)} custom-call(s32[1]{0:T(128)} %bitcast.core, bf16[512,1024]{1,0:T(8,128)(2,1)} %shard_map.28.a0, bf16[512,1024]{1,0:T(8,128)(2,1)} %shard_map.29.a1, bf16[1024,1024]{1,0:T(8,128)(2,1)} %d0.1, bf16[1024,1024]{1,0:T(8,128)(2,1)} %copy-done, f32[1,1024]{1,0:T(1,128)} %bitcast.10, f32[1,1024]{1,0:T(1,128)} %bitcast.12, ...), custom_call_target="tpu_custom_call" | custom-call | flops 10737418240 | bytes 12582912 | tf_op jit(solution)/shard_map/pallas_call | solution.py:187
  54.7 21.0 %all_to_all.16 = bf16[4,128,1024]{2,1,0:T(8,128)(2,1)} all-to-all(bf16[4,128,1024]{2,1,0:T(8,128)(2,1)} %bitcast.8), channel_id=1, replica_groups=mesh['y_lo'=2,'x'=4,'z_hi'=8,'z_lo'=2,'y_hi'=2,'core'=2] {'z_lo','y_hi'}, dimensions={0} | all-to-all | bytes 2097152 | tf_op jit(solution)/shard_map/all_to_all | solution.py:201
  75.7 2.9 %shard_map.31 = bf16[128,1024]{1,0:T(8,128)(2,1)} custom-call(bf16[512,1024]{1,0:T(8,128)(2,1)} %bitcast.6), custom_call_target="tpu_custom_call" | custom-call | bytes 1048576 | tf_op jit(solution)/shard_map/pallas_call | solution.py:50
  78.6 35.5 %all_to_all.17.chunks = bf16[16,8,1024]{2,1,0:T(8,128)(2,1)} all-to-all(bf16[16,8,1024]{2,1,0:T(8,128)(2,1)} %bitcast.7), channel_id=1, replica_groups=mesh['y_lo'=2,'x'=4,'z_hi'=8,'z_lo'=2,'y_hi'=2,'core'=2] {'z_hi','core'}, dimensions={0} | all-to-all | bytes 524288 | tf_op jit(solution)/shard_map/all_to_all | solution.py:203
  114.1 1.7 %shard_map.32 = f32[8,2048]{1,0:T(8,128)} custom-call(bf16[16,8,1024]{2,1,0:T(8,128)(2,1)} %all_to_all.17.chunks), custom_call_target="tpu_custom_call" | custom-call | bytes 262144 | tf_op jit(solution)/shard_map/pallas_call | solution.py:50
  (2 shorter events, 0.0 us)
Async XLA Ops:
  0.0 31.0 %collective-permute-start = (bf16[1024,1024]{1,0:T(8,128)(2,1)}, bf16[1024,1024]{1,0:T(8,128)(2,1)S(1)}, u32[]{:S(2)}, u32[]{:S(2)}) collective-permute-start(bf16[1024,1024]{1,0:T(8,128)(2,1)} %d0.1), channel_id=1, source_target_pairs={{0,1},{1,0},{2,3},{3,2},{4,5},{5,4},{6,7},{7,6},{8,9},{9,8},{10,11... | collective-permute-start | bytes 6291464 | tf_op jit(solution)/shard_map/ppermute | solution.py:172
  9.9 16.6 %collective-permute-start.3 = (bf16[256,1024]{1,0:T(8,128)(2,1)S(1)}, bf16[256,1024]{1,0:T(8,128)(2,1)S(1)}, u32[]{:S(2)}, u32[]{:S(2)}) collective-permute-start(bf16[256,1024]{1,0:T(8,128)(2,1)S(1)} %constant_dynamic-slice_fusion), channel_id=1, source_target_pairs={{192,0},{193,1},{194,2},{195,3},{196,4},{197,5},{198,6},{199,7},{2... | collective-permute-start | bytes 1572872 | tf_op jit(solution)/shard_map/ppermute | solution.py:171
  11.8 16.7 %collective-permute-start.1 = (bf16[256,1024]{1,0:T(8,128)(2,1)S(1)}, bf16[256,1024]{1,0:T(8,128)(2,1)S(1)}, u32[]{:S(2)}, u32[]{:S(2)}) collective-permute-start(bf16[256,1024]{1,0:T(8,128)(2,1)S(1)} %constant_dynamic-slice_fusion), channel_id=1, source_target_pairs={{64,0},{65,1},{66,2},{67,3},{68,4},{69,5},{70,6},{71,7},{72,8},{73... | collective-permute-start | bytes 1572872 | tf_op jit(solution)/shard_map/ppermute | solution.py:170
  26.5 10.9 %copy-start.1 = (bf16[256,1024]{1,0:T(8,128)(2,1)}, bf16[256,1024]{1,0:T(8,128)(2,1)S(1)}, u32[]{:S(2)}) copy-start(bf16[256,1024]{1,0:T(8,128)(2,1)S(1)} %collective-permute-done.3.b3) | copy-start | bytes 1572868
  26.5 10.9 %collective-permute-start.4 = (bf16[128,1024]{1,0:T(8,128)(2,1)S(1)}, bf16[128,1024]{1,0:T(8,128)(2,1)}, u32[]{:S(2)}, u32[]{:S(2)}) collective-permute-start(bf16[128,1024]{1,0:T(8,128)(2,1)S(1)} %slice.9), channel_id=1, source_target_pairs={{448,0},{451,1},{450,2},{449,3},{452,4},{455,5},{454,6},{453,7},{4... | collective-permute-start | bytes 786440 | tf_op jit(solution)/shard_map/ppermute | solution.py:174
  28.5 8.9 %copy-start.2 = (bf16[256,1024]{1,0:T(8,128)(2,1)}, bf16[256,1024]{1,0:T(8,128)(2,1)S(1)}, u32[]{:S(2)}) copy-start(bf16[256,1024]{1,0:T(8,128)(2,1)S(1)} %collective-permute-done.1.b1) | copy-start | bytes 1572868
  28.5 8.9 %collective-permute-start.2 = (bf16[128,1024]{1,0:T(8,128)(2,1)S(1)}, bf16[128,1024]{1,0:T(8,128)(2,1)S(1)}, u32[]{:S(2)}, u32[]{:S(2)}) collective-permute-start(bf16[128,1024]{1,0:T(8,128)(2,1)S(1)} %slice.8), channel_id=1, source_target_pairs={{64,0},{65,1},{66,2},{67,3},{68,4},{69,5},{70,6},{71,7},{72,8},{73... | collective-permute-start | bytes 786440 | tf_op jit(solution)/shard_map/ppermute | solution.py:173
  31.0 1.3 %copy-start = (bf16[1024,1024]{1,0:T(8,128)(2,1)}, bf16[1024,1024]{1,0:T(8,128)(2,1)S(1)}, u32[]{:S(2)}) copy-start(bf16[1024,1024]{1,0:T(8,128)(2,1)S(1)} %collective-permute-done.rows.d1) | copy-start | bytes 6291460
  37.5 0.7 copy-start.3

commit v2 on v0

v2 whole, which is shorter than its diff:
```python
import functools

import jax
import jax.numpy as jnp
from jax import lax
from jax.experimental import pallas as pl
from jax.experimental.pallas import tpu as pltpu
from jax.sharding import Mesh
from jax.sharding import PartitionSpec as P

NAMES = ("y_lo", "x", "z_hi", "z_lo", "y_hi", "core")
SIZES = (2, 4, 8, 2, 2, 2)
KERNEL_VARIANCE = 24.0
D = 1024
ENV = 1024
BLK = 512
HALF = BLK // 2
WIDE = 4 * HALF
TARGET = 14
VMEM = 24 * 1024 * 1024


def flat(y_lo, x, z_hi, z_lo, y_hi, core):
    return ((((y_lo * 4 + x) * 8 + z_hi) * 2 + z_lo) * 2 + y_hi) * 2 + core


def from_group(steps, same_row=False):
    pairs = []
    for y_lo in range(2):
        for x in range(4):
            source = (y_lo * 4 + x + steps) % 8
            s_lo, s_x = divmod(source, 4)
            for z_hi in range(8):
                for z_lo in range(2):
                    for y_hi in range(2):
                        for core in range(2):
                            y = y_hi * 2 + y_lo
                            if s_lo != y_lo and not same_row:
                                y = (y + (1 if core == 0 else -1)) % 4
                            s_hi = y_hi if same_row else y // 2
                            pairs.append((flat(s_lo, s_x, z_hi, z_lo, s_hi, core), flat(y_lo, x, z_hi, z_lo, y_hi, core)))
    return pairs


def call(body, outs, inputs, scratch=(), flops=0):
    size = sum(v.size * v.dtype.itemsize for v in inputs)
    whole = pl.BlockSpec(memory_space=pltpu.VMEM)
    return pl.pallas_call(
        body,
        out_shape=outs,
        in_specs=[pl.BlockSpec(memory_space=pltpu.SMEM) if v.dtype == jnp.int32 else whole for v in inputs],
        out_specs=jax.tree.map(lambda _: whole, outs),
        scratch_shapes=list(scratch),
        compiler_params=pltpu.CompilerParams(vmem_limit_bytes=VMEM),
        cost_estimate=pl.CostEstimate(flops=flops, bytes_accessed=size, transcendentals=0),
    )(*inputs)


def nt(left, right):
    return lax.dot_general(left, right, (((1,), (1,)), ((), ())), preferred_element_type=jnp.float32)


def inverse(values):
    floats = values.astype(jnp.float32)
    return lax.rsqrt(jnp.sum(floats * floats, axis=1, keepdims=True) + 1e-06)


def powered(inner, left_inv, right_inv):
    cosine = inner * left_inv * right_inv
    square = cosine * cosine
    return (KERNEL_VARIANCE * (square * square)).astype(jnp.bfloat16)


def own_kernel(points, rows, out, rows_inv):
    inv = inverse(points[...])
    for i in range(ENV // 256):
        part = slice(i * 256, (i + 1) * 256)
        column = inverse(rows[part, :])
        line = jnp.broadcast_to(column, (256, 128)).T[0:1, :]
        rows_inv[:, part] = line
        out[:, part] = powered(nt(points[...], rows[part, :]), inv, line)


def next_kernel(b, c, d0, d1, e0, e1, k0, k1):
    b_inv, c_inv = inverse(b[...]), inverse(c[...])
    for rows, rows_inv, k in ((d0, e0, k0), (d1, e1, k1)):
        for i in range(ENV // 256):
            part = slice(i * 256, (i + 1) * 256)
            k[0:HALF, part] = powered(nt(b[...], rows[part, :]), b_inv, rows_inv[:, part])
            k[HALF:BLK, part] = powered(nt(c[...], rows[part, :]), c_inv, rows_inv[:, part])


def exponent(largest):
    return jnp.floor(jnp.log2(jnp.maximum(largest, 1e-37)))


def coded(values, half):
    scaled = values * half * half
    scaled = scaled * scaled
    scaled = scaled * scaled
    return scaled * scaled


def marked(scaled, e, rows):
    row = lax.broadcasted_iota(jnp.int32, scaled.shape, 0)
    lane = lax.broadcasted_iota(jnp.int32, scaled.shape, 1)
    number = jnp.broadcast_to(e.astype(jnp.int32) + 128, scaled.shape)
    bit = lax.shift_right_logical(number, jnp.minimum(lane, 30)) & 1
    head = (row % rows == 0) & (lane < 8)
    scaled = jnp.where(head, jnp.maximum(scaled, 1e-35), scaled)
    return jnp.where(head & (bit == 1), -scaled, scaled)


def shift(head):
    floats = head.astype(jnp.float32)
    lane = lax.broadcasted_iota(jnp.int32, floats.shape, 1)
    weight = jnp.left_shift(1, jnp.minimum(lane, 7)).astype(jnp.float32)
    number = jnp.sum(jnp.where((lane < 8) & (floats < 0), weight, 0.0), axis=1, keepdims=True)
    return number - (128 + TARGET)


def decoded(values, add):
    return jnp.exp2(jnp.log2(jnp.abs(values.astype(jnp.float32))) * 0.125 + add)


def gram_kernel(core, a0, a1, n0, n1, d0, d1, e0, e1, b, out, k0, k1, gram):
    mine = pl.ds(pl.multiple_of(core[0] * HALF, HALF), HALF)
    rest = pl.ds(pl.multiple_of((1 - core[0]) * HALF, HALF), HALF)
    inv = inverse(b[...])
    for rows, rows_inv, n, k in ((d0, e0, n0, k0), (d1, e1, n1, k1)):
        k[mine, :] = n[0:HALF, :]
        for i in range(ENV // 256):
            part = slice(i * 256, (i + 1) * 256)
            k[rest, part] = powered(nt(b[...], rows[part, :]), inv, rows_inv[:, part])
    largest = jnp.zeros((1, HALF), jnp.float32)
    for j, (l0, l1, r0, r1, part) in enumerate(
        (
            (a0, a1, a0, a1, mine),
            (a0, a1, n0, n1, slice(0, HALF)),
            (k0, k1, n0, n1, slice(HALF, BLK)),
            (a0, a1, n0, n1, slice(HALF, BLK)),
        )
    ):
        block = nt(l0[...], r0[part, :]) + nt(l1[...], r1[part, :])
        gram[:, j * HALF : (j + 1) * HALF] = block
        largest = jnp.maximum(largest, jnp.max(block, axis=0, keepdims=True))
    e = exponent(jnp.max(largest, axis=1, keepdims=True))
    half = jnp.exp2(0.5 * (TARGET - e))
    for z_hi in range(8):
        for d in range(4):
            values = coded(gram[z_hi * 64 + d * 16 : z_hi * 64 + (d + 1) * 16, :], half)
            to = slice(d * 128 + z_hi * 16, d * 128 + (z_hi + 1) * 16)
            out[to, :] = values.astype(jnp.bfloat16)
            if z_hi == 0:
                out[to, 0:128] = marked(values[:, 0:128], e, 16).astype(jnp.bfloat16)


def middle_kernel(chunks, out):
    total = jnp.zeros((128, WIDE), jnp.float32)
    for s in range(4):
        total = total + decoded(chunks[s * 128 : (s + 1) * 128, :], shift(chunks[s * 128 : s * 128 + 16, 0:128])[0:1])
    e = exponent(jnp.max(jnp.max(total, axis=0, keepdims=True), axis=1, keepdims=True))
    values = coded(total, jnp.exp2(0.5 * (TARGET - e)))
    out[...] = values.astype(jnp.bfloat16)
    out[:, 0:128] = marked(values[:, 0:128], e, 8).astype(jnp.bfloat16)


def last_kernel(tiles, scale, chunks, out):
    for core in range(2):
        adds = [shift(chunks[z_hi * 2 + core, :, 0:128])[0:1] for z_hi in range(8)]
        for tile, to in tiles:
            part = slice(tile * HALF, (tile + 1) * HALF)
            total = jnp.zeros((8, HALF), jnp.float32)
            for z_hi in range(8):
                total = total + decoded(chunks[z_hi * 2 + core, :, part], adds[z_hi])
            out[:, to * BLK + core * HALF : to * BLK + (core + 1) * HALF] = total * scale


def shards(descriptors, sparse_points):
    f32, bf16 = jnp.float32, jnp.bfloat16
    core = lax.axis_index("core")
    swap = [(0, 1), (1, 0)]
    mine = lax.dynamic_slice_in_dim(sparse_points, core * HALF, HALF, 0)
    b = lax.ppermute(mine, NAMES, from_group(1))
    c = lax.ppermute(mine, NAMES, from_group(3))
    other = lax.ppermute(descriptors, "core", swap)

    one = jax.ShapeDtypeStruct((BLK, ENV), bf16)
    line = jax.ShapeDtypeStruct((1, ENV), f32)
    a0, e0 = call(own_kernel, (one, line), (sparse_points, descriptors), flops=2 * BLK * ENV * D)
    a1, e1 = call(own_kernel, (one, line), (sparse_points, other), flops=2 * BLK * ENV * D)
    b, a0, a1 = lax.optimization_barrier((b, a0, a1))
    b_rest = lax.ppermute(b, "core", swap)
    n0, n1 = call(next_kernel, (one, one), (b, c, descriptors, other, e0, e1), flops=4 * BLK * ENV * D)
    sent = call(
        gram_kernel,
        jax.ShapeDtypeStruct((BLK, WIDE), bf16),
        (core.astype(jnp.int32).reshape(1), a0, a1, n0, n1, descriptors, other, e0, e1, b_rest),
        [pltpu.VMEM((BLK, ENV), bf16), pltpu.VMEM((BLK, ENV), bf16), pltpu.VMEM((BLK, WIDE), f32)],
        flops=6 * BLK * ENV * D,
    )
    got = lax.all_to_all(sent, ("z_lo", "y_hi"), 0, 0, tiled=True)
    sent = call(middle_kernel, jax.ShapeDtypeStruct((128, WIDE), bf16), (got,))
    got = lax.all_to_all(sent.reshape(16, 8, WIDE), ("z_hi", "core"), 0, 0, tiled=True)
    scale = 1.0 / (ENV * 64)
    later = call(functools.partial(last_kernel, ((2, 0),), scale), jax.ShapeDtypeStruct((8, BLK), f32), (got,))
    later = lax.ppermute(later, NAMES, from_group(-1, same_row=True))
    tiles = ((0, 0), (1, 1), (3, 3))
    out = call(functools.partial(last_kernel, tiles, scale), jax.ShapeDtypeStruct((8, 4 * BLK), f32), (got,))
    return lax.dynamic_update_slice(out, later, (0, 2 * BLK))


def solution(mesh):
    fine = Mesh(mesh.devices.reshape(SIZES), NAMES)
    return jax.shard_map(
        shards,
        mesh=fine,
        in_specs=(P(("z_hi", "z_lo", "y_hi", "core"), None), P(("y_lo", "x"), None)),
        out_specs=P(NAMES, None),
        check_vma=False,
    )
```

time: 334 us -> 99.7 us (0.30)
  the two profiles are of different devices: /device:TPU:2 before, /device:TPU:1 now
where the time goes in v2:
time: 99.7 us; the launch traced here: 99.2 us
  blocking collectives  55.4 us (56%)
  starting transfers between devices  17.2 us (17%)
  Pallas kernels  12.5 us (13%)
  waiting for transfers between devices  9.48 us (10%)
  local copies, waits for them, and re-layouts  4.5 us (5%)
    all_to_all x1, blocking collectives, shards(): lax.all_to_all(sent.reshape(16, 8, WIDE), ('z_hi', 'core'), 0, 0, tiled=T...  37.6 us
    all_to_all x1, blocking collectives, shards(): got = lax.all_to_all(sent, ('z_lo', 'y_hi'), 0, 0, tiled=True)  17.8 us
    pallas_call x7, Pallas kernels, call(): pl.pallas_call(body, out_shape=outs, in_specs=[pl.BlockSpec(memory_space=...  12.5 us
    ppermute x1, starting transfers between devices, shards(): other = lax.ppermute(descriptors, 'core', swap)  8.78 us
    ppermute x1, waiting for transfers between devices, shards(): b = lax.ppermute(mine, NAMES, from_group(1))  5.14 us
    ppermute x1, waiting for transfers between devices, shards(): later = lax.ppermute(later, NAMES, from_group(-1, same_row=True))  3.89 us
    unnamed x6, local copies, waits for them, and re-layouts  2.82 us
    ppermute x1, starting transfers between devices, shards(): b_rest = lax.ppermute(b, 'core', swap)  2.69 us
  transfers between devices with their start and end apart: 5, of which 3 were waited for; matrix products, arithmetic and copies ran while one was open for 1% of the time, Pallas kernels for 7%

profile of v2, /device:TPU:1, one launch (start us, length us, event | category | flops | bytes accessed | tf_op | source)
XLA Modules:
  0.0 99.2 jit_solution(12968997433102978843)
XLA Ops:
  0.0 8.8 %collective-permute-start.1 = (bf16[1024,1024]{1,0:T(8,128)(2,1)}, bf16[1024,1024]{1,0:T(8,128)(2,1)S(1)}, u32[]{:S(2)}, u32[]{:S(2)}) collective-permute-start(bf16[1024,1024]{1,0:T(8,128)(2,1)} %d0.3), channel_id=1, source_target_pairs={{0,1},{1,0},{2,3},{3,2},{4,5},{5,4},{6,7},{7,6},{8,9},{9,8},{10,11... | collective-permute-start | bytes 6291464 | tf_op jit(solution)/shard_map/ppermute | solution.py:186
  8.8 1.1 %constant_dynamic-slice_fusion = bf16[256,1024]{1,0:T(8,128)(2,1)S(1)} fusion(bf16[512,1024]{1,0:T(8,128)(2,1)} %points.3, s32[]{:T(128)S(6)} %select_n.3), kind=kLoop, calls=%fused_computation.1 | loop fusion | bytes 1048580 | tf_op jit(solution)/shard_map/dynamic_slice | solution.py:183
  9.9 1.9 %collective-permute-start = (bf16[256,1024]{1,0:T(8,128)(2,1)S(1)}, bf16[256,1024]{1,0:T(8,128)(2,1)S(1)}, u32[]{:S(2)}, u32[]{:S(2)}) collective-permute-start(bf16[256,1024]{1,0:T(8,128)(2,1)S(1)} %constant_dynamic-slice_fusion), channel_id=1, source_target_pairs={{64,0},{65,1},{66,2},{67,3},{68,4},{69,5},{70,6},{71,7},{72,8},{73... | collective-permute-start | bytes 1572872 | tf_op jit(solution)/shard_map/ppermute | solution.py:184
  11.8 1.9 %collective-permute-start.2 = (bf16[256,1024]{1,0:T(8,128)(2,1)S(1)}, bf16[256,1024]{1,0:T(8,128)(2,1)S(1)}, u32[]{:S(2)}, u32[]{:S(2)}) collective-permute-start(bf16[256,1024]{1,0:T(8,128)(2,1)S(1)} %constant_dynamic-slice_fusion), channel_id=1, source_target_pairs={{192,0},{193,1},{194,2},{195,3},{196,4},{197,5},{198,6},{199,7},{2... | collective-permute-start | bytes 1572872 | tf_op jit(solution)/shard_map/ppermute | solution.py:185
  13.7 0.0 copy-start
  13.7 1.2 %copy-done = bf16[512,1024]{1,0:T(8,128)(2,1)S(1)} copy-done((bf16[512,1024]{1,0:T(8,128)(2,1)S(1)}, bf16[512,1024]{1,0:T(8,128)(2,1)}, u32[]{:S(2)}) %copy-start) | copy-done | bytes 1048600
  15.0 0.0 copy-start.1
  15.0 1.6 %copy-done.1 = bf16[1024,1024]{1,0:T(8,128)(2,1)S(1)} copy-done((bf16[1024,1024]{1,0:T(8,128)(2,1)S(1)}, bf16[1024,1024]{1,0:T(8,128)(2,1)}, u32[]{:S(2)}) %copy-start.1) | copy-done | bytes 2097176
  16.6 1.8 %shard_map.28 = (bf16[512,1024]{1,0:T(8,128)(2,1)S(1)}, f32[1,1024]{1,0:T(1,128)S(1)}) custom-call(bf16[512,1024]{1,0:T(8,128)(2,1)S(1)} %copy-done, bf16[1024,1024]{1,0:T(8,128)(2,1)S(1)} %copy-done.1), custom_call_target="tpu_custom_call" | custom-call | flops 1073741824 | bytes 3145728 | tf_op jit(solution)/shard_map/pallas_call | solution.py:48
  18.3 0.0 copy-start.2
  18.4 0.0 collective-permute-done.1.rows.d1
  18.4 1.8 %shard_map.29 = (bf16[512,1024]{1,0:T(8,128)(2,1)S(1)}, f32[1,1024]{1,0:T(1,128)S(1)}) custom-call(bf16[512,1024]{1,0:T(8,128)(2,1)S(1)} %copy-done, bf16[1024,1024]{1,0:T(8,128)(2,1)S(1)} %collective-permute-done.1.rows.d1), custom_call_target="tpu_custom_call" | custom-call | flops 1073741824 | bytes 3145728 | tf_op jit(solution)/shard_map/pallas_call | solution.py:48
  20.2 5.1 %collective-permute-done.b = bf16[256,1024]{1,0:T(8,128)(2,1)S(1)} collective-permute-done((bf16[256,1024]{1,0:T(8,128)(2,1)S(1)}, bf16[256,1024]{1,0:T(8,128)(2,1)S(1)}, u32[]{:S(2)}, u32[]{:S(2)}) %collective-permute-start) | collective-permute-done | bytes 524320 | tf_op jit(solution)/shard_map/ppermute | solution.py:184
  25.3 2.7 %collective-permute-start.3 = (bf16[256,1024]{1,0:T(8,128)(2,1)S(1)}, bf16[256,1024]{1,0:T(8,128)(2,1)S(1)}, u32[]{:S(2)}, u32[]{:S(2)}) collective-permute-start(bf16[256,1024]{1,0:T(8,128)(2,1)S(1)} %collective-permute-done.b), channel_id=1, source_target_pairs={{0,1},{1,0},{2,3},{3,2},{4,5},{5,4},{6,7},{7,6},{8,9},{9,8},{10,11... | collective-permute-start | bytes 1572872 | tf_op jit(solution)/shard_map/ppermute | solution.py:193
  28.0 0.4 collective-permute-done.2.c
  28.5 0.0 copy-done.2
  28.5 2.9 %shard_map.30 = (bf16[512,1024]{1,0:T(8,128)(2,1)S(1)}, bf16[512,1024]{1,0:T(8,128)(2,1)S(1)}) custom-call(bf16[256,1024]{1,0:T(8,128)(2,1)S(1)} %collective-permute-done.b, bf16[256,1024]{1,0:T(8,128)(2,1)S(1)} %collective-permute-done.2.c, bf16[1024,1024]{1,0:T(8,128)(2,1)S(1)} %copy-done.2, bf16[1024,1024]{1,0:T(8,128)(2,1)S(1)} %collective-permute-done.1.rows.d1, ...), custom_call_target="tpu_custom_call" | custom-call | flops 2147483648 | bytes 5251072 | tf_op jit(solution)/shard_map/pallas_call | solution.py:48
  31.3 0.0 collective-permute-done.3.b
  31.3 4.3 %shard_map.31 = bf16[512,1024]{1,0:T(8,128)(2,1)S(1)} custom-call(s32[1]{0:T(128)} %bitcast.core, bf16[512,1024]{1,0:T(8,128)(2,1)S(1)} %get-tuple-element.16.a0, bf16[512,1024]{1,0:T(8,128)(2,1)S(1)} %get-tuple-element.17.a1, bf16[512,1024]{1,0:T(8,128)(2,1)S(1)} %get-tuple-element.21.n0, bf16[512,1024]{1,0:T(8,128)(2,1)S(1)} %get-tuple-element.22.n1, ...), custom_call_target="tpu_custom_call" | custom-call | flops 3221225472 | bytes 8921092 | tf_op jit(solution)/shard_map/pallas_call | solution.py:48
  35.6 17.8 %all_to_all.16 = bf16[4,128,1024]{2,1,0:T(8,128)(2,1)S(1)} all-to-all(bf16[4,128,1024]{2,1,0:T(8,128)(2,1)S(1)} %bitcast.6), channel_id=1, replica_groups=mesh['y_lo'=2,'x'=4,'z_hi'=8,'z_lo'=2,'y_hi'=2,'core'=2] {'z_lo','y_hi'}, dimensions={0} | all-to-all | bytes 2097152 | tf_op jit(solution)/shard_map/all_to_all | solution.py:202
  53.4 0.9 shard_map.32
  54.3 37.6 %all_to_all.17.chunks = bf16[16,8,1024]{2,1,0:T(8,128)(2,1)S(1)} all-to-all(bf16[16,8,1024]{2,1,0:T(8,128)(2,1)S(1)} %bitcast.5), channel_id=1, replica_groups=mesh['y_lo'=2,'x'=4,'z_hi'=8,'z_lo'=2,'y_hi'=2,'core'=2] {'z_hi','core'}, dimensions={0} | all-to-all | bytes 524288 | tf_op jit(solution)/shard_map/all_to_all | solution.py:204
  91.9 0.1 shard_map.34
  92.0 1.9 %collective-permute-start.4 = (f32[8,512]{1,0:T(8,128)S(1)}, f32[8,512]{1,0:T(8,128)S(1)}, u32[]{:S(2)}, u32[]{:S(2)}) collective-permute-start(f32[8,512]{1,0:T(8,128)S(1)} %shard_map.34), channel_id=1, source_target_pairs={{448,0},{449,1},{450,2},{451,3},{452,4},{453,5},{454,6},{455,7},{4... | collective-permute-start | bytes 49160 | tf_op jit(solution)/shard_map/ppermute | solution.py:207
  94.0 0.8 shard_map.33
  94.7 3.9 %collective-permute-done.4 = f32[8,512]{1,0:T(8,128)S(1)} collective-permute-done((f32[8,512]{1,0:T(8,128)S(1)}, f32[8,512]{1,0:T(8,128)S(1)}, u32[]{:S(2)}, u32[]{:S(2)}) %collective-permute-start.4) | collective-permute-done | bytes 16416 | tf_op jit(solution)/shard_map/ppermute | solution.py:207
  98.6 0.6 constant_dynamic-update-slice_fusion
Async XLA Ops:
  0.0 18.4 %collective-permute-start.1 = (bf16[1024,1024]{1,0:T(8,128)(2,1)}, bf16[1024,1024]{1,0:T(8,128)(2,1)S(1)}, u32[]{:S(2)}, u32[]{:S(2)}) collective-permute-start(bf16[1024,1024]{1,0:T(8,128)(2,1)} %d0.3), channel_id=1, source_target_pairs={{0,1},{1,0},{2,3},{3,2},{4,5},{5,4},{6,7},{7,6},{8,9},{9,8},{10,11... | collective-permute-start | bytes 6291464 | tf_op jit(solution)/shard_map/ppermute | solution.py:186
  9.9 15.4 %collective-permute-start = (bf16[256,1024]{1,0:T(8,128)(2,1)S(1)}, bf16[256,1024]{1,0:T(8,128)(2,1)S(1)}, u32[]{:S(2)}, u32[]{:S(2)}) collective-permute-start(bf16[256,1024]{1,0:T(8,128)(2,1)S(1)} %constant_dynamic-slice_fusion), channel_id=1, source_target_pairs={{64,0},{65,1},{66,2},{67,3},{68,4},{69,5},{70,6},{71,7},{72,8},{73... | collective-permute-start | bytes 1572872 | tf_op jit(solution)/shard_map/ppermute | solution.py:184
  11.8 16.6 %collective-permute-start.2 = (bf16[256,1024]{1,0:T(8,128)(2,1)S(1)}, bf16[256,1024]{1,0:T(8,128)(2,1)S(1)}, u32[]{:S(2)}, u32[]{:S(2)}) collective-permute-start(bf16[256,1024]{1,0:T(8,128)(2,1)S(1)} %constant_dynamic-slice_fusion), channel_id=1, source_target_pairs={{192,0},{193,1},{194,2},{195,3},{196,4},{197,5},{198,6},{199,7},{2... | collective-permute-start | bytes 1572872 | tf_op jit(solution)/shard_map/ppermute | solution.py:185
  13.7 1.2 %copy-start = (bf16[512,1024]{1,0:T(8,128)(2,1)S(1)}, bf16[512,1024]{1,0:T(8,128)(2,1)}, u32[]{:S(2)}) copy-start(bf16[512,1024]{1,0:T(8,128)(2,1)} %points.3) | copy-start | bytes 3145732
  15.0 1.6 %copy-start.1 = (bf16[1024,1024]{1,0:T(8,128)(2,1)S(1)}, bf16[1024,1024]{1,0:T(8,128)(2,1)}, u32[]{:S(2)}) copy-start(bf16[1024,1024]{1,0:T(8,128)(2,1)} %d0.3) | copy-start | bytes 6291460
  18.3 10.1 %copy-start.2 = (bf16[1024,1024]{1,0:T(8,128)(2,1)S(1)}, bf16[1024,1024]{1,0:T(8,128)(2,1)}, u32[]{:S(2)}) copy-start(bf16[1024,1024]{1,0:T(8,128)(2,1)} %d0.3) | copy-start | bytes 6291460
  25.3 6.0 %collective-permute-start.3 = (bf16[256,1024]{1,0:T(8,128)(2,1)S(1)}, bf16[256,1024]{1,0:T(8,128)(2,1)S(1)}, u32[]{:S(2)}, u32[]{:S(2)}) collective-permute-start(bf16[256,1024]{1,0:T(8,128)(2,1)S(1)} %collective-permute-done.b), channel_id=1, source_target_pairs={{0,1},{1,0},{2,3},{3,2},{4,5},{5,4},{6,7},{7,6},{8,9},{9,8},{10,11... | collective-permute-start | bytes 1572872 | tf_op jit(solution)/shard_map/ppermute | solution.py:193
  92.0 6.6 %collective-permute-start.4 = (f32[8,512]{1,0:T(8,128)S(1)}, f32[8,512]{1,0:T(8,128)S(1)}, u32[]{:S(2)}, u32[]{:S(2)}) collective-permute-start(f32[8,512]{1,0:T(8,128)S(1)} %shard_map.34), channel_id=1, source_target_pairs={{448,0},{449,1},{450,2},{451,3},{452,4},{453,5},{454,6},{455,7},{4... | collective-permute-start | bytes 49160 | tf_op jit(solution)/shard_map/ppermute | solution.py:207

commit v3 on v2

v3 whole, which is shorter than its diff:
```python
import functools

import jax
import jax.numpy as jnp
from jax import lax
from jax.experimental import pallas as pl
from jax.experimental.pallas import tpu as pltpu
from jax.sharding import Mesh
from jax.sharding import PartitionSpec as P

NAMES = ("y_lo", "x", "z_hi", "z_lo", "y_hi", "core")
SIZES = (2, 4, 8, 2, 2, 2)
KERNEL_VARIANCE = 24.0
D = 1024
ENV = 1024
BLK = 512
HALF = BLK // 2
WIDE = 4 * HALF
TARGET = 14
VMEM = 24 * 1024 * 1024


def flat(y_lo, x, z_hi, z_lo, y_hi, core):
    return ((((y_lo * 4 + x) * 8 + z_hi) * 2 + z_lo) * 2 + y_hi) * 2 + core


def from_group(steps, same_row=False):
    pairs = []
    for y_lo in range(2):
        for x in range(4):
            source = (y_lo * 4 + x + steps) % 8
            s_lo, s_x = divmod(source, 4)
            for z_hi in range(8):
                for z_lo in range(2):
                    for y_hi in range(2):
                        for core in range(2):
                            y = y_hi * 2 + y_lo
                            if s_lo != y_lo and not same_row:
                                y = (y + (1 if core == 0 else -1)) % 4
                            s_hi = y_hi if same_row else y // 2
                            pairs.append((flat(s_lo, s_x, z_hi, z_lo, s_hi, core), flat(y_lo, x, z_hi, z_lo, y_hi, core)))
    return pairs


def call(body, outs, inputs, scratch=(), flops=0):
    size = sum(v.size * v.dtype.itemsize for v in inputs)
    whole = pl.BlockSpec(memory_space=pltpu.VMEM)
    return pl.pallas_call(
        body,
        out_shape=outs,
        in_specs=[pl.BlockSpec(memory_space=pltpu.SMEM) if v.dtype == jnp.int32 else whole for v in inputs],
        out_specs=jax.tree.map(lambda _: whole, outs),
        scratch_shapes=list(scratch),
        compiler_params=pltpu.CompilerParams(vmem_limit_bytes=VMEM),
        cost_estimate=pl.CostEstimate(flops=flops, bytes_accessed=size, transcendentals=0),
    )(*inputs)


def nt(left, right):
    return lax.dot_general(left, right, (((1,), (1,)), ((), ())), preferred_element_type=jnp.float32)


def inverse(values):
    floats = values.astype(jnp.float32)
    return lax.rsqrt(jnp.sum(floats * floats, axis=1, keepdims=True) + 1e-06)


def powered(inner, left_inv, right_inv):
    cosine = inner * left_inv * right_inv
    square = cosine * cosine
    return (KERNEL_VARIANCE * (square * square)).astype(jnp.bfloat16)


def half_kernel(core, points, out, sem):
    mine = pl.ds(pl.multiple_of(core[0] * HALF, HALF), HALF)
    copy = pltpu.make_async_copy(points.at[mine, :], out, sem)
    copy.start()
    copy.wait()


def own_columns(points, inv, rows, part, out, rows_inv):
    line = jnp.broadcast_to(inverse(rows[part, :]), (256, 128)).T[0:1, :]
    rows_inv[:, part] = line
    out[:, part] = powered(nt(points[...], rows[part, :]), inv, line)


def first_kernel(points_far, rows_far, out, rows_inv, points, rows, sems):
    parts = [slice(i * 256, (i + 1) * 256) for i in range(ENV // 256)]
    copies = [pltpu.make_async_copy(points_far, points, sems.at[4])]
    copies += [pltpu.make_async_copy(rows_far.at[p, :], rows.at[p, :], sems.at[i]) for i, p in enumerate(parts)]
    for copy in copies:
        copy.start()
    copies[0].wait()
    inv = inverse(points[...])
    for copy, part in zip(copies[1:], parts):
        copy.wait()
        own_columns(points, inv, rows, part, out, rows_inv)


def tile(left, right):
    return nt(left[0], right[0]) + nt(left[1], right[1])


def fill(points, inv, rows, rows_inv, out):
    for i in range(ENV // 256):
        part = slice(i * 256, (i + 1) * 256)
        out[:, part] = powered(nt(points[...], rows[part, :]), inv, rows_inv[:, part])


def second_kernel(core, points, rows, a0, a1, rows_inv, gram):
    inv = inverse(points[...])
    for i in range(ENV // 256):
        own_columns(points, inv, rows, slice(i * 256, (i + 1) * 256), a1, rows_inv)
    mine = pl.ds(pl.multiple_of(core[0] * HALF, HALF), HALF)
    gram[...] = tile((a0[...], a1[...]), (a0[mine, :], a1[mine, :]))


def next_kernel(b, d0, d1, e0, e1, a0, a1, b0, b1, gram):
    inv = inverse(b[...])
    fill(b, inv, d0, e0, b0)
    fill(b, inv, d1, e1, b1)
    gram[...] = tile((a0[...], a1[...]), (b0[...], b1[...]))


def exponent(largest):
    return jnp.floor(jnp.log2(jnp.maximum(largest, 1e-37)))


def coded(values, half):
    scaled = values * half * half
    scaled = scaled * scaled
    scaled = scaled * scaled
    return scaled * scaled


def marked(scaled, e, rows):
    row = lax.broadcasted_iota(jnp.int32, scaled.shape, 0)
    lane = lax.broadcasted_iota(jnp.int32, scaled.shape, 1)
    number = jnp.broadcast_to(e.astype(jnp.int32) + 128, scaled.shape)
    bit = lax.shift_right_logical(number, jnp.minimum(lane, 30)) & 1
    head = (row % rows == 0) & (lane < 8)
    scaled = jnp.where(head, jnp.maximum(scaled, 1e-35), scaled)
    return jnp.where(head & (bit == 1), -scaled, scaled)


def shift(head):
    floats = head.astype(jnp.float32)
    lane = lax.broadcasted_iota(jnp.int32, floats.shape, 1)
    weight = jnp.left_shift(1, jnp.minimum(lane, 7)).astype(jnp.float32)
    number = jnp.sum(jnp.where((lane < 8) & (floats < 0), weight, 0.0), axis=1, keepdims=True)
    return number - (128 + TARGET)


def decoded(values, add):
    return jnp.exp2(jnp.log2(jnp.abs(values.astype(jnp.float32))) * 0.125 + add)


def gram_kernel(core, g_aa, g_ab, a0, a1, b0, b1, c, rest, d0, d1, e0, e1, out, c0, c1, k0, k1, gram):
    mine = pl.ds(pl.multiple_of(core[0] * HALF, HALF), HALF)
    others = pl.ds(pl.multiple_of((1 - core[0]) * HALF, HALF), HALF)
    c_inv, rest_inv = inverse(c[...]), inverse(rest[...])
    for rows, rows_inv, out_c, old, k in ((d0, e0, c0, b0, k0), (d1, e1, c1, b1, k1)):
        fill(c, c_inv, rows, rows_inv, out_c)
        k[mine, :] = old[...]
        for i in range(ENV // 256):
            part = slice(i * 256, (i + 1) * 256)
            k[others, part] = powered(nt(rest[...], rows[part, :]), rest_inv, rows_inv[:, part])
    columns = (c0[...], c1[...])
    ac = tile((a0[...], a1[...]), columns)
    bc = tile((k0[...], k1[...]), columns)
    gram[:, 0:HALF] = ac
    gram[:, HALF:BLK] = bc
    largest = jnp.maximum(
        jnp.maximum(jnp.max(ac, axis=0, keepdims=True), jnp.max(bc, axis=0, keepdims=True)),
        jnp.maximum(jnp.max(g_aa[...], axis=0, keepdims=True), jnp.max(g_ab[...], axis=0, keepdims=True)),
    )
    e = exponent(jnp.max(largest, axis=1, keepdims=True))
    half = jnp.exp2(0.5 * (TARGET - e))
    for d in range(8):
        for pair in range(4):
            starts = [(2 * pair + i) * 64 + d * 8 for i in range(2)]
            to = slice(d * 64 + pair * 16, d * 64 + (pair + 1) * 16)
            column = 0
            for source in (g_aa, g_ab, gram):
                width = source.shape[1]
                values = coded(jnp.concatenate([source[r : r + 8, :] for r in starts], axis=0), half)
                out[to, column : column + width] = values.astype(jnp.bfloat16)
                if pair == 0 and column == 0:
                    out[to, 0:128] = marked(values[:, 0:128], e, 16).astype(jnp.bfloat16)
                column += width


def middle_kernel(chunks, out):
    totals = []
    for core in range(2):
        total = jnp.zeros((64, WIDE), jnp.float32)
        for s in range(core, 8, 2):
            add = shift(chunks[s * 64 : s * 64 + 16, 0:128])[0:1]
            total = total + decoded(chunks[s * 64 : (s + 1) * 64, :], add)
        totals.append(total)
    largest = jnp.maximum(jnp.max(totals[0], axis=0, keepdims=True), jnp.max(totals[1], axis=0, keepdims=True))
    e = exponent(jnp.max(largest, axis=1, keepdims=True))
    half = jnp.exp2(0.5 * (TARGET - e))
    for core in range(2):
        values = coded(totals[core], half)
        out[:, core * WIDE : (core + 1) * WIDE] = values.astype(jnp.bfloat16)
        if core == 0:
            out[:, 0:128] = marked(values[:, 0:128], e, 8).astype(jnp.bfloat16)


def last_kernel(tiles, scale, chunks, out):
    adds = [shift(chunks[z_hi, :, 0:128])[0:1] for z_hi in range(8)]
    for core in range(2):
        for source, to in tiles:
            part = slice(core * WIDE + source * HALF, core * WIDE + (source + 1) * HALF)
            total = jnp.zeros((8, HALF), jnp.float32)
            for z_hi in range(8):
                total = total + decoded(chunks[z_hi, :, part], adds[z_hi])
            out[:, to * BLK + core * HALF : to * BLK + (core + 1) * HALF] = total * scale


def shards(descriptors, sparse_points):
    f32, bf16 = jnp.float32, jnp.bfloat16
    core = lax.axis_index("core")
    number = core.astype(jnp.int32).reshape(1)
    swap = [(0, 1), (1, 0)]
    one = jax.ShapeDtypeStruct((BLK, ENV), bf16)
    half = jax.ShapeDtypeStruct((HALF, ENV), bf16)
    line = jax.ShapeDtypeStruct((1, ENV), f32)
    gram = jax.ShapeDtypeStruct((BLK, HALF), f32)
    work = 2 * BLK * ENV * D
    far = pl.BlockSpec(memory_space=pltpu.HBM)
    points_far = pltpu.with_memory_space_constraint(sparse_points, pltpu.HBM)
    rows_far = pltpu.with_memory_space_constraint(descriptors, pltpu.HBM)
    whole = pl.BlockSpec(memory_space=pltpu.VMEM)
    mine = pl.pallas_call(
        half_kernel,
        out_shape=jax.ShapeDtypeStruct((HALF, D), bf16),
        in_specs=[pl.BlockSpec(memory_space=pltpu.SMEM), far],
        out_specs=whole,
        scratch_shapes=[pltpu.SemaphoreType.DMA],
        compiler_params=pltpu.CompilerParams(vmem_limit_bytes=VMEM),
    )(number, points_far)
    b = lax.ppermute(mine, NAMES, from_group(1))
    c = lax.ppermute(mine, NAMES, from_group(3))
    a0, e0 = pl.pallas_call(
        first_kernel,
        out_shape=(one, line),
        in_specs=[far, far],
        out_specs=(whole, whole),
        scratch_shapes=[pltpu.VMEM((BLK, D), bf16), pltpu.VMEM((ENV, D), bf16), pltpu.SemaphoreType.DMA((5,))],
        compiler_params=pltpu.CompilerParams(vmem_limit_bytes=VMEM),
        cost_estimate=pl.CostEstimate(flops=work, bytes_accessed=3 * 2**20, transcendentals=0),
    )(points_far, rows_far)
    other = lax.ppermute(descriptors, "core", swap)
    a1, e1, g_aa = call(second_kernel, (one, line, gram), (number, sparse_points, other, a0), flops=work * 3 // 2)
    b, a1, g_aa = lax.optimization_barrier((b, a1, g_aa))
    rest = lax.ppermute(b, "core", swap)
    b0, b1, g_ab = call(next_kernel, (half, half, gram), (b, descriptors, other, e0, e1, a0, a1), flops=work * 3 // 2)
    sent = call(
        gram_kernel,
        jax.ShapeDtypeStruct((BLK, WIDE), bf16),
        (number, g_aa, g_ab, a0, a1, b0, b1, c, rest, descriptors, other, e0, e1),
        [pltpu.VMEM((HALF, ENV), bf16)] * 2 + [pltpu.VMEM((BLK, ENV), bf16)] * 2 + [pltpu.VMEM((BLK, BLK), f32)],
        flops=work * 3,
    )
    got = lax.all_to_all(sent, ("z_lo", "y_hi", "core"), 0, 0, tiled=True)
    sent = call(middle_kernel, jax.ShapeDtypeStruct((64, 2 * WIDE), bf16), (got,))
    got = lax.all_to_all(sent.reshape(8, 8, 2 * WIDE), "z_hi", 0, 0, tiled=True)
    scale = 1.0 / (ENV * 64)
    ahead = call(functools.partial(last_kernel, ((3, 0),), scale), jax.ShapeDtypeStruct((8, BLK), f32), (got,))
    ahead = lax.ppermute(ahead, NAMES, from_group(-1, same_row=True))
    tiles = ((0, 0), (1, 1), (2, 3))
    out = call(functools.partial(last_kernel, tiles, scale), jax.ShapeDtypeStruct((8, 4 * BLK), f32), (got,))
    return lax.dynamic_update_slice(out, ahead, (0, 2 * BLK))


def solution(mesh):
    fine = Mesh(mesh.devices.reshape(SIZES), NAMES)
    return jax.shard_map(
        shards,
        mesh=fine,
        in_specs=(P(("z_hi", "z_lo", "y_hi", "core"), None), P(("y_lo", "x"), None)),
        out_specs=P(NAMES, None),
        check_vma=False,
    )
```

time: 99.7 us -> 95.3 us (0.956)
  the two profiles are of different devices: /device:TPU:1 before, /device:TPU:8 now
where the time goes in v3:
time: 95.3 us; the launch traced here: 94.9 us
  blocking collectives  54.3 us (57%)
  starting transfers between devices  17.4 us (18%)
  Pallas kernels  17.4 us (18%)
  waiting for transfers between devices  5.06 us (5%)
    all_to_all x1, blocking collectives, shards(): got = lax.all_to_all(sent.reshape(8, 8, 2 * WIDE), 'z_hi', 0, 0, tiled=True)  35.1 us
    all_to_all x1, blocking collectives, shards(): got = lax.all_to_all(sent, ('z_lo', 'y_hi', 'core'), 0, 0, tiled=True)  19.1 us
    pallas_call x6, Pallas kernels, call(): pl.pallas_call(body, out_shape=outs, in_specs=[pl.BlockSpec(memory_space=...  11.9 us
    ppermute x1, starting transfers between devices, shards(): c = lax.ppermute(mine, NAMES, from_group(3))  6.55 us
    ppermute x1, waiting for transfers between devices, shards(): ahead = lax.ppermute(ahead, NAMES, from_group(-1, same_row=True))  5.05 us
    ppermute x1, starting transfers between devices, shards(): b = lax.ppermute(mine, NAMES, from_group(1))  4.68 us
    pallas_call x1, Pallas kernels, shards(): pl.pallas_call(first_kernel, out_shape=(one, line), in_specs=[far, far],...  4.48 us
    ppermute x1, starting transfers between devices, shards(): ahead = lax.ppermute(ahead, NAMES, from_group(-1, same_row=True))  2.32 us
  transfers between devices with their start and end apart: 5, of which 1 were waited for; matrix products, arithmetic and copies ran while one was open for 0% of the time, Pallas kernels for 13%

profile of v3, /device:TPU:8, one launch (start us, length us, event | category | flops | bytes accessed | tf_op | source)
XLA Modules:
  0.0 94.9 jit_solution(18182674285203589380)
XLA Ops:
  0.0 1.9 %collective-permute-start.1 = (bf16[1024,1024]{1,0:T(8,128)(2,1)}, bf16[1024,1024]{1,0:T(8,128)(2,1)S(1)}, u32[]{:S(2)}, u32[]{:S(2)}) collective-permute-start(bf16[1024,1024]{1,0:T(8,128)(2,1)} %d0.3), channel_id=1, source_target_pairs={{0,1},{1,0},{2,3},{3,2},{4,5},{5,4},{6,7},{7,6},{8,9},{9,8},{10,11... | collective-permute-start | bytes 6291464 | tf_op jit(solution)/shard_map/ppermute | solution.py:255
  1.9 1.1 %shard_map.28 = bf16[256,1024]{1,0:T(8,128)(2,1)S(1)} custom-call(s32[1]{0:T(128)} %bitcast.core, bf16[512,1024]{1,0:T(8,128)(2,1)} %points.3), custom_call_target="tpu_custom_call" | custom-call | tf_op jit(solution)/shard_map/pallas_call | solution.py:236
  3.0 0.0 copy-start.1
  3.0 4.7 %collective-permute-start = (bf16[256,1024]{1,0:T(8,128)(2,1)S(1)}, bf16[256,1024]{1,0:T(8,128)(2,1)S(1)}, u32[]{:S(2)}, u32[]{:S(2)}) collective-permute-start(bf16[256,1024]{1,0:T(8,128)(2,1)S(1)} %shard_map.28), channel_id=1, source_target_pairs={{64,0},{65,1},{66,2},{67,3},{68,4},{69,5},{70,6},{71,7},{72,8},{73... | collective-permute-start | bytes 1572872 | tf_op jit(solution)/shard_map/ppermute | solution.py:244
  7.7 6.5 %collective-permute-start.2 = (bf16[256,1024]{1,0:T(8,128)(2,1)S(1)}, bf16[256,1024]{1,0:T(8,128)(2,1)S(1)}, u32[]{:S(2)}, u32[]{:S(2)}) collective-permute-start(bf16[256,1024]{1,0:T(8,128)(2,1)S(1)} %shard_map.28), channel_id=1, source_target_pairs={{192,0},{193,1},{194,2},{195,3},{196,4},{197,5},{198,6},{199,7},{2... | collective-permute-start | bytes 1572872 | tf_op jit(solution)/shard_map/ppermute | solution.py:245
  14.2 4.5 %shard_map.29 = (bf16[512,1024]{1,0:T(8,128)(2,1)S(1)}, f32[1,1024]{1,0:T(1,128)S(1)}) custom-call(bf16[512,1024]{1,0:T(8,128)(2,1)} %points.3, bf16[1024,1024]{1,0:T(8,128)(2,1)} %d0.3), custom_call_target="tpu_custom_call" | custom-call | flops 1073741824 | bytes 3145728 | tf_op jit(solution)/shard_map/pallas_call | solution.py:246
  18.7 0.0 collective-permute-done.1.rows.d1
  18.7 0.0 copy-done.1
  18.8 0.0 copy-start
  18.8 3.5 %shard_map.30 = (bf16[512,1024]{1,0:T(8,128)(2,1)S(1)}, f32[1,1024]{1,0:T(1,128)S(1)}, f32[512,256]{1,0:T(8,128)S(1)}) custom-call(s32[1]{0:T(128)} %bitcast.core, bf16[512,1024]{1,0:T(8,128)(2,1)S(1)} %copy-done.1, bf16[1024,1024]{1,0:T(8,128)(2,1)S(1)} %collective-permute-done.1.rows.d1, bf16[512,1024]{1,0:T(8,128)(2,1)S(1)} %get-tuple-element.16.a0), custom_call_target="tpu_custom_call" | custom-call | flops 1610612736 | bytes 4194308 | tf_op jit(solution)/shard_map/pallas_call | solution.py:48
  22.3 0.0 collective-permute-done.b
  22.3 1.9 %collective-permute-start.3 = (bf16[256,1024]{1,0:T(8,128)(2,1)S(1)}, bf16[256,1024]{1,0:T(8,128)(2,1)S(1)}, u32[]{:S(2)}, u32[]{:S(2)}) collective-permute-start(bf16[256,1024]{1,0:T(8,128)(2,1)S(1)} %collective-permute-done.b), channel_id=1, source_target_pairs={{0,1},{1,0},{2,3},{3,2},{4,5},{5,4},{6,7},{7,6},{8,9},{9,8},{10,11... | collective-permute-start | bytes 1572872 | tf_op jit(solution)/shard_map/ppermute | solution.py:258
  24.2 0.0 copy-done
  24.2 2.1 %shard_map.31 = (bf16[256,1024]{1,0:T(8,128)(2,1)S(1)}, bf16[256,1024]{1,0:T(8,128)(2,1)S(1)}, f32[512,256]{1,0:T(8,128)S(1)}) custom-call(bf16[256,1024]{1,0:T(8,128)(2,1)S(1)} %collective-permute-done.b, bf16[1024,1024]{1,0:T(8,128)(2,1)S(1)} %copy-done, bf16[1024,1024]{1,0:T(8,128)(2,1)S(1)} %collective-permute-done.1.rows.d1, ...), custom_call_target="tpu_custom_call" | custom-call | flops 1610612736 | bytes 6823936 | tf_op jit(solution)/shard_map/pallas_call | solution.py:48
  26.3 0.0 collective-permute-done.2.c
  26.3 0.0 collective-permute-done.3.rest
  26.3 4.6 %shard_map.32 = bf16[512,1024]{1,0:T(8,128)(2,1)S(1)} custom-call(s32[1]{0:T(128)} %bitcast.core, f32[512,256]{1,0:T(8,128)S(1)} %get-tuple-element.19.g_aa, f32[512,256]{1,0:T(8,128)S(1)} %get-tuple-element.24.g_ab, bf16[512,1024]{1,0:T(8,128)(2,1)S(1)} %get-tuple-element.16.a0, bf16[512,1024]{1,0:T(8,128)(2,1)S(1)} %get-tuple-element.23.a1, ...), custom_call_target="tpu_custom_call" | custom-call | flops 3221225472 | bytes 9445380 | tf_op jit(solution)/shard_map/pallas_call | solution.py:48
  30.9 19.1 %all_to_all.16 = bf16[8,64,1024]{2,1,0:T(8,128)(2,1)S(1)} all-to-all(bf16[8,64,1024]{2,1,0:T(8,128)(2,1)S(1)} %bitcast.6), channel_id=1, replica_groups=mesh['y_lo'=2,'x'=4,'z_hi'=8,'z_lo'=2,'y_hi'=2,'core'=2] {'z_lo','y_hi',..., dimensions={0} | all-to-all | bytes 2097152 | tf_op jit(solution)/shard_map/all_to_all | solution.py:267
  50.1 0.8 shard_map.33
  50.9 35.1 %all_to_all.17.chunks = bf16[8,8,2048]{2,1,0:T(8,128)(2,1)S(1)} all-to-all(bf16[8,8,2048]{2,1,0:T(8,128)(2,1)S(1)} %bitcast.5), channel_id=1, replica_groups=mesh['y_lo'=2,'x'=4,'z_hi'=8,'z_lo'=2,'y_hi'=2,'core'=2] {'z_hi'}, dimensions={0} | all-to-all | bytes 524288 | tf_op jit(solution)/shard_map/all_to_all | solution.py:269
  86.0 0.1 shard_map.35
  86.2 2.3 %collective-permute-start.4 = (f32[8,512]{1,0:T(8,128)S(1)}, f32[8,512]{1,0:T(8,128)S(1)}, u32[]{:S(2)}, u32[]{:S(2)}) collective-permute-start(f32[8,512]{1,0:T(8,128)S(1)} %shard_map.35), channel_id=1, source_target_pairs={{448,0},{449,1},{450,2},{451,3},{452,4},{453,5},{454,6},{455,7},{4... | collective-permute-start | bytes 49160 | tf_op jit(solution)/shard_map/ppermute | solution.py:272
  88.5 0.8 shard_map.34
  89.3 5.1 %collective-permute-done.4 = f32[8,512]{1,0:T(8,128)S(1)} collective-permute-done((f32[8,512]{1,0:T(8,128)S(1)}, f32[8,512]{1,0:T(8,128)S(1)}, u32[]{:S(2)}, u32[]{:S(2)}) %collective-permute-start.4) | collective-permute-done | bytes 16416 | tf_op jit(solution)/shard_map/ppermute | solution.py:272
  94.3 0.6 constant_dynamic-update-slice_fusion
Async XLA Ops:
  0.0 18.7 %collective-permute-start.1 = (bf16[1024,1024]{1,0:T(8,128)(2,1)}, bf16[1024,1024]{1,0:T(8,128)(2,1)S(1)}, u32[]{:S(2)}, u32[]{:S(2)}) collective-permute-start(bf16[1024,1024]{1,0:T(8,128)(2,1)} %d0.3), channel_id=1, source_target_pairs={{0,1},{1,0},{2,3},{3,2},{4,5},{5,4},{6,7},{7,6},{8,9},{9,8},{10,11... | collective-permute-start | bytes 6291464 | tf_op jit(solution)/shard_map/ppermute | solution.py:255
  3.0 15.8 %copy-start.1 = (bf16[512,1024]{1,0:T(8,128)(2,1)S(1)}, bf16[512,1024]{1,0:T(8,128)(2,1)}, u32[]{:S(2)}) copy-start(bf16[512,1024]{1,0:T(8,128)(2,1)} %points.3) | copy-start | bytes 3145732
  3.0 19.3 %collective-permute-start = (bf16[256,1024]{1,0:T(8,128)(2,1)S(1)}, bf16[256,1024]{1,0:T(8,128)(2,1)S(1)}, u32[]{:S(2)}, u32[]{:S(2)}) collective-permute-start(bf16[256,1024]{1,0:T(8,128)(2,1)S(1)} %shard_map.28), channel_id=1, source_target_pairs={{64,0},{65,1},{66,2},{67,3},{68,4},{69,5},{70,6},{71,7},{72,8},{73... | collective-permute-start | bytes 1572872 | tf_op jit(solution)/shard_map/ppermute | solution.py:244
  7.7 18.6 %collective-permute-start.2 = (bf16[256,1024]{1,0:T(8,128)(2,1)S(1)}, bf16[256,1024]{1,0:T(8,128)(2,1)S(1)}, u32[]{:S(2)}, u32[]{:S(2)}) collective-permute-start(bf16[256,1024]{1,0:T(8,128)(2,1)S(1)} %shard_map.28), channel_id=1, source_target_pairs={{192,0},{193,1},{194,2},{195,3},{196,4},{197,5},{198,6},{199,7},{2... | collective-permute-start | bytes 1572872 | tf_op jit(solution)/shard_map/ppermute | solution.py:245
  18.8 5.5 %copy-start = (bf16[1024,1024]{1,0:T(8,128)(2,1)S(1)}, bf16[1024,1024]{1,0:T(8,128)(2,1)}, u32[]{:S(2)}) copy-start(bf16[1024,1024]{1,0:T(8,128)(2,1)} %d0.3) | copy-start | bytes 6291460
  22.3 4.1 %collective-permute-start.3 = (bf16[256,1024]{1,0:T(8,128)(2,1)S(1)}, bf16[256,1024]{1,0:T(8,128)(2,1)S(1)}, u32[]{:S(2)}, u32[]{:S(2)}) collective-permute-start(bf16[256,1024]{1,0:T(8,128)(2,1)S(1)} %collective-permute-done.b), channel_id=1, source_target_pairs={{0,1},{1,0},{2,3},{3,2},{4,5},{5,4},{6,7},{7,6},{8,9},{9,8},{10,11... | collective-permute-start | bytes 1572872 | tf_op jit(solution)/shard_map/ppermute | solution.py:258
  86.2 8.1 %collective-permute-start.4 = (f32[8,512]{1,0:T(8,128)S(1)}, f32[8,512]{1,0:T(8,128)S(1)}, u32[]{:S(2)}, u32[]{:S(2)}) collective-permute-start(f32[8,512]{1,0:T(8,128)S(1)} %shard_map.35), channel_id=1, source_target_pairs={{448,0},{449,1},{450,2},{451,3},{452,4},{453,5},{454,6},{455,7},{4... | collective-permute-start | bytes 49160 | tf_op jit(solution)/shard_map/ppermute | solution.py:272

commit v4 on v3

v4 whole, which is shorter than its diff:
```python
import functools

import jax
import jax.numpy as jnp
from jax import lax
from jax.experimental import pallas as pl
from jax.experimental.pallas import tpu as pltpu
from jax.sharding import Mesh
from jax.sharding import PartitionSpec as P

NAMES = ("y_lo", "x", "z_hi", "z_lo", "y_hi", "core")
SIZES = (2, 4, 8, 2, 2, 2)
KERNEL_VARIANCE = 24.0
D = 1024
ENV = 1024
BLK = 512
HALF = BLK // 2
WIDE = 4 * HALF
TARGET = 14
VMEM = 24 * 1024 * 1024


def flat(y_lo, x, z_hi, z_lo, y_hi, core):
    return ((((y_lo * 4 + x) * 8 + z_hi) * 2 + z_lo) * 2 + y_hi) * 2 + core


def from_group(steps):
    pairs = []
    for y_lo in range(2):
        for x in range(4):
            for z_hi in range(8):
                for z_lo in range(2):
                    for y_hi in range(2):
                        for core in range(2):
                            s_lo, s_x = divmod((y_lo * 4 + x + steps[core]) % 8, 4)
                            y = y_hi * 2 + y_lo
                            if s_lo != y_lo:
                                y = (y + (1 if core == 0 else -1)) % 4
                            pairs.append((flat(s_lo, s_x, z_hi, z_lo, y // 2, core), flat(y_lo, x, z_hi, z_lo, y_hi, core)))
    return pairs


def call(body, outs, inputs, scratch=(), flops=0):
    size = sum(v.size * v.dtype.itemsize for v in inputs)
    whole = pl.BlockSpec(memory_space=pltpu.VMEM)
    return pl.pallas_call(
        body,
        out_shape=outs,
        in_specs=[pl.BlockSpec(memory_space=pltpu.SMEM) if v.dtype == jnp.int32 else whole for v in inputs],
        out_specs=jax.tree.map(lambda _: whole, outs),
        scratch_shapes=list(scratch),
        compiler_params=pltpu.CompilerParams(vmem_limit_bytes=VMEM),
        cost_estimate=pl.CostEstimate(flops=flops, bytes_accessed=size, transcendentals=0),
    )(*inputs)


def nt(left, right):
    return lax.dot_general(left, right, (((1,), (1,)), ((), ())), preferred_element_type=jnp.float32)


def inverse(values):
    floats = values.astype(jnp.float32)
    return lax.rsqrt(jnp.sum(floats * floats, axis=1, keepdims=True) + 1e-06)


def powered(inner, left_inv, right_inv):
    cosine = inner * left_inv * right_inv
    square = cosine * cosine
    return (KERNEL_VARIANCE * (square * square)).astype(jnp.bfloat16)


def halves_kernel(core, points, out, rest, sems):
    copies = []
    for i, (half, to) in enumerate(((core[0], out), (1 - core[0], rest))):
        rows = pl.ds(pl.multiple_of(half * HALF, HALF), HALF)
        copies.append(pltpu.make_async_copy(points.at[rows, :], to, sems.at[i]))
    for copy in copies:
        copy.start()
    for copy in copies:
        copy.wait()


def own_kernel(mine, rest, rows, out, rows_inv):
    mine_inv, rest_inv = inverse(mine[...]), inverse(rest[...])
    for i in range(ENV // 256):
        part = slice(i * 256, (i + 1) * 256)
        line = jnp.broadcast_to(inverse(rows[part, :]), (256, 128)).T[0:1, :]
        rows_inv[:, part] = line
        out[0:HALF, part] = powered(nt(mine[...], rows[part, :]), mine_inv, line)
        out[HALF:BLK, part] = powered(nt(rest[...], rows[part, :]), rest_inv, line)


def tile(left, right):
    return nt(left[0], right[0]) + nt(left[1], right[1])


def fill(points, inv, rows, rows_inv, out):
    for i in range(ENV // 256):
        part = slice(i * 256, (i + 1) * 256)
        out[:, part] = powered(nt(points[...], rows[part, :]), inv, rows_inv[:, part])


def second_kernel(mine, rest, rows, a1, a0, rows_inv, gram):
    own_kernel(mine, rest, rows, a0, rows_inv)
    gram[...] = tile((a0[...], a1[...]), (a0[0:HALF, :], a1[0:HALF, :]))


def next_kernel(b, d0, d1, e0, e1, a0, a1, gram, b0, b1):
    inv = inverse(b[...])
    fill(b, inv, d0, e0, b0)
    fill(b, inv, d1, e1, b1)
    gram[...] = tile((a0[...], a1[...]), (b0[...], b1[...]))


def exponent(largest):
    return jnp.floor(jnp.log2(jnp.maximum(largest, 1e-37)))


def coded(values, half):
    scaled = values * half * half
    scaled = scaled * scaled
    scaled = scaled * scaled
    return scaled * scaled


def marked(scaled, e, rows):
    row = lax.broadcasted_iota(jnp.int32, scaled.shape, 0)
    lane = lax.broadcasted_iota(jnp.int32, scaled.shape, 1)
    number = jnp.broadcast_to(e.astype(jnp.int32) + 128, scaled.shape)
    bit = lax.shift_right_logical(number, jnp.minimum(lane, 30)) & 1
    head = (row % rows == 0) & (lane < 8)
    scaled = jnp.where(head, jnp.maximum(scaled, 1e-35), scaled)
    return jnp.where(head & (bit == 1), -scaled, scaled)


def shift(head):
    floats = head.astype(jnp.float32)
    lane = lax.broadcasted_iota(jnp.int32, floats.shape, 1)
    weight = jnp.left_shift(1, jnp.minimum(lane, 7)).astype(jnp.float32)
    number = jnp.sum(jnp.where((lane < 8) & (floats < 0), weight, 0.0), axis=1, keepdims=True)
    return number - (128 + TARGET)


def decoded(values, add):
    return jnp.exp2(jnp.log2(jnp.abs(values.astype(jnp.float32))) * 0.125 + add)


def gram_kernel(core, g0, near, rest, a0, a1, b, d0, d1, e0, e1, out, b0, b1, g2):
    next_kernel(b, d0, d1, e0, e1, a0, a1, g2, b0, b1)
    sources = (g0, near, rest, g2)
    largest = jnp.zeros((1, HALF), jnp.float32)
    for source in sources:
        largest = jnp.maximum(largest, jnp.max(source[...], axis=0, keepdims=True))
    e = exponent(jnp.max(largest, axis=1, keepdims=True))
    half = jnp.exp2(0.5 * (TARGET - e))
    for d in range(8):
        for pair in range(4):
            starts = [lax.rem((2 * pair + i) * 64 + core[0] * HALF, BLK) + d * 8 for i in range(2)]
            starts = [pl.multiple_of(r, 8) for r in starts]
            to = slice(d * 64 + pair * 16, d * 64 + (pair + 1) * 16)
            for j, source in enumerate(sources):
                values = coded(jnp.concatenate([source[pl.ds(r, 8), :] for r in starts], axis=0), half)
                out[to, j * HALF : (j + 1) * HALF] = values.astype(jnp.bfloat16)
                if pair == 0 and j == 0:
                    out[to, 0:128] = marked(values[:, 0:128], e, 16).astype(jnp.bfloat16)


def middle_kernel(chunks, out):
    totals = []
    for core in range(2):
        total = jnp.zeros((64, WIDE), jnp.float32)
        for s in range(core, 8, 2):
            add = shift(chunks[s * 64 : s * 64 + 16, 0:128])[0:1]
            total = total + decoded(chunks[s * 64 : (s + 1) * 64, :], add)
        totals.append(total)
    largest = jnp.maximum(jnp.max(totals[0], axis=0, keepdims=True), jnp.max(totals[1], axis=0, keepdims=True))
    e = exponent(jnp.max(largest, axis=1, keepdims=True))
    half = jnp.exp2(0.5 * (TARGET - e))
    for core in range(2):
        values = coded(totals[core], half)
        out[:, core * WIDE : (core + 1) * WIDE] = values.astype(jnp.bfloat16)
        if core == 0:
            out[:, 0:128] = marked(values[:, 0:128], e, 8).astype(jnp.bfloat16)


def last_kernel(scale, chunks, out):
    adds = [shift(chunks[z_hi, :, 0:128])[0:1] for z_hi in range(8)]
    for core in range(2):
        near = 1 if core == 0 else 3
        for i, (j, half) in enumerate(((0, core), (near, core), (near, 1 - core), (2, core))):
            part = slice(core * WIDE + i * HALF, core * WIDE + (i + 1) * HALF)
            total = jnp.zeros((8, HALF), jnp.float32)
            for z_hi in range(8):
                total = total + decoded(chunks[z_hi, :, part], adds[z_hi])
            out[:, j * BLK + half * HALF : j * BLK + (half + 1) * HALF] = total * scale


def shards(descriptors, sparse_points):
    f32, bf16 = jnp.float32, jnp.bfloat16
    core = lax.axis_index("core")
    number = core.astype(jnp.int32).reshape(1)
    swap = [(0, 1), (1, 0)]
    one = jax.ShapeDtypeStruct((BLK, ENV), bf16)
    half = pltpu.VMEM((HALF, ENV), bf16)
    line = jax.ShapeDtypeStruct((1, ENV), f32)
    gram = jax.ShapeDtypeStruct((BLK, HALF), f32)
    work = 2 * BLK * ENV * D
    far = pl.BlockSpec(memory_space=pltpu.HBM)
    points_far = pltpu.with_memory_space_constraint(sparse_points, pltpu.HBM)
    whole = pl.BlockSpec(memory_space=pltpu.VMEM)
    mine, rest = pl.pallas_call(
        halves_kernel,
        out_shape=(jax.ShapeDtypeStruct((HALF, D), bf16), jax.ShapeDtypeStruct((HALF, D), bf16)),
        in_specs=[pl.BlockSpec(memory_space=pltpu.SMEM), far],
        out_specs=(whole, whole),
        scratch_shapes=[pltpu.SemaphoreType.DMA((2,))],
        compiler_params=pltpu.CompilerParams(vmem_limit_bytes=VMEM),
    )(number, points_far)
    near = [lax.ppermute(v, NAMES, from_group((1, 3))) for v in (mine, rest)]
    other = lax.ppermute(descriptors, "core", swap)
    a1, e1 = call(own_kernel, (one, line), (mine, rest, other), flops=work)
    a0, e0, g_aa = call(second_kernel, (one, line, gram), (mine, rest, descriptors, a1), flops=work * 3 // 2)
    near[0], e0 = lax.optimization_barrier((near[0], e0))
    far_points = lax.ppermute(near[0], NAMES, from_group((1, -1)))
    tiles = []
    for points in near:
        inputs = (points, descriptors, other, e0, e1, a0, a1)
        tiles.append(call(next_kernel, gram, inputs, [half, half], flops=work * 3 // 2))
    inputs = (number, g_aa, *tiles, a0, a1, far_points, descriptors, other, e0, e1)
    scratch = [half, half, pltpu.VMEM((BLK, HALF), f32)]
    sent = call(gram_kernel, jax.ShapeDtypeStruct((BLK, WIDE), bf16), inputs, scratch, flops=work * 3 // 2)
    got = lax.all_to_all(sent, ("z_lo", "y_hi", "core"), 0, 0, tiled=True)
    sent = call(middle_kernel, jax.ShapeDtypeStruct((64, 2 * WIDE), bf16), (got,))
    got = lax.all_to_all(sent.reshape(8, 8, 2 * WIDE), "z_hi", 0, 0, tiled=True)
    scale = 1.0 / (ENV * 64)
    out = jax.ShapeDtypeStruct((8, 4 * BLK), f32)
    return call(functools.partial(last_kernel, scale), out, (got,))


def solution(mesh):
    fine = Mesh(mesh.devices.reshape(SIZES), NAMES)
    return jax.shard_map(
        shards,
        mesh=fine,
        in_specs=(P(("z_hi", "z_lo", "y_hi", "core"), None), P(("y_lo", "x"), None)),
        out_specs=P(NAMES, None),
        check_vma=False,
    )
```

time: 95.3 us -> 92.6 us (0.972)
  the two profiles are of different devices: /device:TPU:8 before, /device:TPU:14 now
where the time goes in v4:
time: 92.6 us; the launch traced here: 92.3 us
  blocking collectives  58.4 us (63%)
  Pallas kernels  13.7 us (15%)
  waiting for transfers between devices  10.9 us (12%)
  starting transfers between devices  9.13 us (10%)
    all_to_all x1, blocking collectives, shards(): got = lax.all_to_all(sent.reshape(8, 8, 2 * WIDE), 'z_hi', 0, 0, tiled=True)  35.2 us
    all_to_all x1, blocking collectives, shards(): got = lax.all_to_all(sent, ('z_lo', 'y_hi', 'core'), 0, 0, tiled=True)  23.2 us
    pallas_call x7, Pallas kernels, call(): pl.pallas_call(body, out_shape=outs, in_specs=[pl.BlockSpec(memory_space=...  12.5 us
    ppermute x1, waiting for transfers between devices, shards(): far_points = lax.ppermute(near[0], NAMES, from_group((1, -1)))  5.52 us
    ppermute x2, waiting for transfers between devices, shards(): near = [lax.ppermute(v, NAMES, from_group((1, 3))) for v in (mine, rest)]  5.36 us
    ppermute x2, starting transfers between devices, shards(): near = [lax.ppermute(v, NAMES, from_group((1, 3))) for v in (mine, rest)]  5.31 us
    ppermute x1, starting transfers between devices, shards(): other = lax.ppermute(descriptors, 'core', swap)  1.91 us
    ppermute x1, starting transfers between devices, shards(): far_points = lax.ppermute(near[0], NAMES, from_group((1, -1)))  1.91 us
  transfers between devices with their start and end apart: 4, of which 3 were waited for; matrix products, arithmetic and copies ran while one was open for 0% of the time, Pallas kernels for 10%

profile of v4, /device:TPU:14, one launch (start us, length us, event | category | flops | bytes accessed | tf_op | source)
XLA Modules:
  0.0 92.3 jit_solution(13580820658364227079)
XLA Ops:
  0.0 1.9 %collective-permute-start = (bf16[1024,1024]{1,0:T(8,128)(2,1)}, bf16[1024,1024]{1,0:T(8,128)(2,1)S(1)}, u32[]{:S(2)}, u32[]{:S(2)}) collective-permute-start(bf16[1024,1024]{1,0:T(8,128)(2,1)} %d0.5), channel_id=1, source_target_pairs={{0,1},{1,0},{2,3},{3,2},{4,5},{5,4},{6,7},{7,6},{8,9},{9,8},{10,11... | collective-permute-start | bytes 6291464 | tf_op jit(solution)/shard_map/ppermute | solution.py:220
  1.9 1.2 %shard_map.28 = (bf16[256,1024]{1,0:T(8,128)(2,1)S(1)}, bf16[256,1024]{1,0:T(8,128)(2,1)S(1)}) custom-call(s32[1]{0:T(128)} %bitcast.core, bf16[512,1024]{1,0:T(8,128)(2,1)} %points.1), custom_call_target="tpu_custom_call" | custom-call | tf_op jit(solution)/shard_map/pallas_call | solution.py:211
  3.1 0.0 copy-start
  3.2 2.9 %collective-permute-start.1 = (bf16[256,1024]{1,0:T(8,128)(2,1)S(1)}, bf16[256,1024]{1,0:T(8,128)(2,1)S(1)}, u32[]{:S(2)}, u32[]{:S(2)}) collective-permute-start(bf16[256,1024]{1,0:T(8,128)(2,1)S(1)} %get-tuple-element.14.mine), channel_id=1, source_target_pairs={{64,0},{193,1},{66,2},{195,3},{68,4},{197,5},{70,6},{199,7},{72,8}... | collective-permute-start | bytes 1572872 | tf_op jit(solution)/shard_map/ppermute | solution.py:219
  6.0 2.4 %collective-permute-start.2 = (bf16[256,1024]{1,0:T(8,128)(2,1)S(1)}, bf16[256,1024]{1,0:T(8,128)(2,1)S(1)}, u32[]{:S(2)}, u32[]{:S(2)}) collective-permute-start(bf16[256,1024]{1,0:T(8,128)(2,1)S(1)} %get-tuple-element.15.rest), channel_id=1, source_target_pairs={{64,0},{193,1},{66,2},{195,3},{68,4},{197,5},{70,6},{199,7},{72,8}... | collective-permute-start | bytes 1572872 | tf_op jit(solution)/shard_map/ppermute | solution.py:219
  8.5 0.0 collective-permute-done.rows.d1
  8.5 1.9 %shard_map.29 = (bf16[512,1024]{1,0:T(8,128)(2,1)S(1)}, f32[1,1024]{1,0:T(1,128)S(1)}) custom-call(bf16[256,1024]{1,0:T(8,128)(2,1)S(1)} %get-tuple-element.14.mine, bf16[256,1024]{1,0:T(8,128)(2,1)S(1)} %get-tuple-element.15.rest, bf16[1024,1024]{1,0:T(8,128)(2,1)S(1)} %collective-permute-done.rows.d1), custom_call_target="tpu_custom_call" | custom-call | flops 1073741824 | bytes 3145728 | tf_op jit(solution)/shard_map/pallas_call | solution.py:46
  10.4 0.0 copy-done
  10.4 2.4 %shard_map.30 = (bf16[512,1024]{1,0:T(8,128)(2,1)S(1)}, f32[1,1024]{1,0:T(1,128)S(1)}, f32[512,256]{1,0:T(8,128)S(1)}) custom-call(bf16[256,1024]{1,0:T(8,128)(2,1)S(1)} %get-tuple-element.14.mine, bf16[256,1024]{1,0:T(8,128)(2,1)S(1)} %get-tuple-element.15.rest, bf16[1024,1024]{1,0:T(8,128)(2,1)S(1)} %copy-done, bf16[512,1024]{1,0:T(8,128)(2,1)S(1)} %get-tuple-element.16.a1), custom_call_target="tpu_custom_call" | custom-call | flops 1610612736 | bytes 4194304 | tf_op jit(solution)/shard_map/pallas_call | solution.py:46
  12.8 3.7 %collective-permute-done.1.b = bf16[256,1024]{1,0:T(8,128)(2,1)S(1)} collective-permute-done((bf16[256,1024]{1,0:T(8,128)(2,1)S(1)}, bf16[256,1024]{1,0:T(8,128)(2,1)S(1)}, u32[]{:S(2)}, u32[]{:S(2)}) %collective-permute-start.1) | collective-permute-done | bytes 524320 | tf_op jit(solution)/shard_map/ppermute | solution.py:219
  16.5 1.9 %collective-permute-start.3 = (bf16[256,1024]{1,0:T(8,128)(2,1)S(1)}, bf16[256,1024]{1,0:T(8,128)(2,1)S(1)}, u32[]{:S(2)}, u32[]{:S(2)}) collective-permute-start(bf16[256,1024]{1,0:T(8,128)(2,1)S(1)} %collective-permute-done.1.b), channel_id=1, source_target_pairs={{64,0},{451,1},{66,2},{449,3},{68,4},{455,5},{70,6},{453,7},{72,8}... | collective-permute-start | bytes 1572872 | tf_op jit(solution)/shard_map/ppermute | solution.py:224
  18.4 2.0 %shard_map.31.near = f32[512,256]{1,0:T(8,128)S(1)} custom-call(bf16[256,1024]{1,0:T(8,128)(2,1)S(1)} %collective-permute-done.1.b, bf16[1024,1024]{1,0:T(8,128)(2,1)S(1)} %copy-done, bf16[1024,1024]{1,0:T(8,128)(2,1)S(1)} %collective-permute-done.rows.d1, f32[1,1024]{1,0:T(1,128)S(1)} %get-tuple-element.20.e0, f32[1,1024]{1,0:T(1,128)S(1)} %get-tuple-element.21.e1, ...), custom_call_target="tpu_custom_call" | custom-call | flops 1610612736 | bytes 6823936 | tf_op jit(solution)/shard_map/pallas_call | solution.py:46
  20.4 1.7 %collective-permute-done.2.b = bf16[256,1024]{1,0:T(8,128)(2,1)S(1)} collective-permute-done((bf16[256,1024]{1,0:T(8,128)(2,1)S(1)}, bf16[256,1024]{1,0:T(8,128)(2,1)S(1)}, u32[]{:S(2)}, u32[]{:S(2)}) %collective-permute-start.2) | collective-permute-done | bytes 524320 | tf_op jit(solution)/shard_map/ppermute | solution.py:219
  22.1 2.0 %shard_map.32.rest = f32[512,256]{1,0:T(8,128)S(1)} custom-call(bf16[256,1024]{1,0:T(8,128)(2,1)S(1)} %collective-permute-done.2.b, bf16[1024,1024]{1,0:T(8,128)(2,1)S(1)} %copy-done, bf16[1024,1024]{1,0:T(8,128)(2,1)S(1)} %collective-permute-done.rows.d1, f32[1,1024]{1,0:T(1,128)S(1)} %get-tuple-element.20.e0, f32[1,1024]{1,0:T(1,128)S(1)} %get-tuple-element.21.e1, ...), custom_call_target="tpu_custom_call" | custom-call | flops 1610612736 | bytes 6823936 | tf_op jit(solution)/shard_map/pallas_call | solution.py:46
  24.1 5.5 %collective-permute-done.3.b = bf16[256,1024]{1,0:T(8,128)(2,1)S(1)} collective-permute-done((bf16[256,1024]{1,0:T(8,128)(2,1)S(1)}, bf16[256,1024]{1,0:T(8,128)(2,1)S(1)}, u32[]{:S(2)}, u32[]{:S(2)}) %collective-permute-start.3) | collective-permute-done | bytes 524320 | tf_op jit(solution)/shard_map/ppermute | solution.py:224
  29.7 2.6 %shard_map.33 = bf16[512,1024]{1,0:T(8,128)(2,1)S(1)} custom-call(s32[1]{0:T(128)} %bitcast.core, f32[512,256]{1,0:T(8,128)S(1)} %get-tuple-element.17.g0, f32[512,256]{1,0:T(8,128)S(1)} %shard_map.31.near, f32[512,256]{1,0:T(8,128)S(1)} %shard_map.32.rest, bf16[512,1024]{1,0:T(8,128)(2,1)S(1)} %get-tuple-element.22.a0, ...), custom_call_target="tpu_custom_call" | custom-call | flops 1610612736 | bytes 8396804 | tf_op jit(solution)/shard_map/pallas_call | solution.py:46
  32.2 23.2 %all_to_all.16 = bf16[8,64,1024]{2,1,0:T(8,128)(2,1)S(1)} all-to-all(bf16[8,64,1024]{2,1,0:T(8,128)(2,1)S(1)} %bitcast.5), channel_id=1, replica_groups=mesh['y_lo'=2,'x'=4,'z_hi'=8,'z_lo'=2,'y_hi'=2,'core'=2] {'z_lo','y_hi',..., dimensions={0} | all-to-all | bytes 2097152 | tf_op jit(solution)/shard_map/all_to_all | solution.py:232
  55.4 0.8 shard_map.34
  56.3 35.2 %all_to_all.17.chunks = bf16[8,8,2048]{2,1,0:T(8,128)(2,1)S(1)} all-to-all(bf16[8,8,2048]{2,1,0:T(8,128)(2,1)S(1)} %bitcast.6), channel_id=1, replica_groups=mesh['y_lo'=2,'x'=4,'z_hi'=8,'z_lo'=2,'y_hi'=2,'core'=2] {'z_hi'}, dimensions={0} | all-to-all | bytes 524288 | tf_op jit(solution)/shard_map/all_to_all | solution.py:234
  91.5 0.8 shard_map.35
Async XLA Ops:
  0.0 8.5 %collective-permute-start = (bf16[1024,1024]{1,0:T(8,128)(2,1)}, bf16[1024,1024]{1,0:T(8,128)(2,1)S(1)}, u32[]{:S(2)}, u32[]{:S(2)}) collective-permute-start(bf16[1024,1024]{1,0:T(8,128)(2,1)} %d0.5), channel_id=1, source_target_pairs={{0,1},{1,0},{2,3},{3,2},{4,5},{5,4},{6,7},{7,6},{8,9},{9,8},{10,11... | collective-permute-start | bytes 6291464 | tf_op jit(solution)/shard_map/ppermute | solution.py:220
  3.1 7.3 %copy-start = (bf16[1024,1024]{1,0:T(8,128)(2,1)S(1)}, bf16[1024,1024]{1,0:T(8,128)(2,1)}, u32[]{:S(2)}) copy-start(bf16[1024,1024]{1,0:T(8,128)(2,1)} %d0.5) | copy-start | bytes 6291460
  3.2 13.3 %collective-permute-start.1 = (bf16[256,1024]{1,0:T(8,128)(2,1)S(1)}, bf16[256,1024]{1,0:T(8,128)(2,1)S(1)}, u32[]{:S(2)}, u32[]{:S(2)}) collective-permute-start(bf16[256,1024]{1,0:T(8,128)(2,1)S(1)} %get-tuple-element.14.mine), channel_id=1, source_target_pairs={{64,0},{193,1},{66,2},{195,3},{68,4},{197,5},{70,6},{199,7},{72,8}... | collective-permute-start | bytes 1572872 | tf_op jit(solution)/shard_map/ppermute | solution.py:219
  6.0 16.1 %collective-permute-start.2 = (bf16[256,1024]{1,0:T(8,128)(2,1)S(1)}, bf16[256,1024]{1,0:T(8,128)(2,1)S(1)}, u32[]{:S(2)}, u32[]{:S(2)}) collective-permute-start(bf16[256,1024]{1,0:T(8,128)(2,1)S(1)} %get-tuple-element.15.rest), channel_id=1, source_target_pairs={{64,0},{193,1},{66,2},{195,3},{68,4},{197,5},{70,6},{199,7},{72,8}... | collective-permute-start | bytes 1572872 | tf_op jit(solution)/shard_map/ppermute | solution.py:219
  16.5 13.2 %collective-permute-start.3 = (bf16[256,1024]{1,0:T(8,128)(2,1)S(1)}, bf16[256,1024]{1,0:T(8,128)(2,1)S(1)}, u32[]{:S(2)}, u32[]{:S(2)}) collective-permute-start(bf16[256,1024]{1,0:T(8,128)(2,1)S(1)} %collective-permute-done.1.b), channel_id=1, source_target_pairs={{64,0},{451,1},{66,2},{449,3},{68,4},{455,5},{70,6},{453,7},{72,8}... | collective-permute-start | bytes 1572872 | tf_op jit(solution)/shard_map/ppermute | solution.py:224

commit v5 on v4

--- a/solution.py
+++ b/solution.py
@@ -217,7 +217,8 @@
         compiler_params=pltpu.CompilerParams(vmem_limit_bytes=VMEM),
     )(number, points_far)
     near = [lax.ppermute(v, NAMES, from_group((1, 3))) for v in (mine, rest)]
-    other = lax.ppermute(descriptors, "core", swap)
+    mine, rest, rows = lax.optimization_barrier((mine, rest, descriptors))
+    other = lax.ppermute(rows, "core", swap)
     a1, e1 = call(own_kernel, (one, line), (mine, rest, other), flops=work)
     a0, e0, g_aa = call(second_kernel, (one, line, gram), (mine, rest, descriptors, a1), flops=work * 3 // 2)
     near[0], e0 = lax.optimization_barrier((near[0], e0))

time: 92.6 us -> 92.6 us (level)
  transfers between devices with their start and end apart: 4 -> 4, of which waited for: 3 -> 3; matrix products, arithmetic and copies ran while one was open for 0% -> 0% of each run, Pallas kernels for 10% -> 9%
where the time goes in v5:
time: 92.6 us; the launch traced here: 92.3 us
  blocking collectives  58.4 us (63%)
  Pallas kernels  13.7 us (15%)
  waiting for transfers between devices  10.9 us (12%)
  starting transfers between devices  9.14 us (10%)
    all_to_all x1, blocking collectives, shards(): got = lax.all_to_all(sent.reshape(8, 8, 2 * WIDE), 'z_hi', 0, 0, tiled=True)  35.2 us
    all_to_all x1, blocking collectives, shards(): got = lax.all_to_all(sent, ('z_lo', 'y_hi', 'core'), 0, 0, tiled=True)  23.2 us
    pallas_call x7, Pallas kernels, call(): pl.pallas_call(body, out_shape=outs, in_specs=[pl.BlockSpec(memory_space=...  12.5 us
    ppermute x1, waiting for transfers between devices, shards(): far_points = lax.ppermute(near[0], NAMES, from_group((1, -1)))  5.54 us
    ppermute x2, waiting for transfers between devices, shards(): near = [lax.ppermute(v, NAMES, from_group((1, 3))) for v in (mine, rest)]  5.34 us
    ppermute x2, starting transfers between devices, shards(): near = [lax.ppermute(v, NAMES, from_group((1, 3))) for v in (mine, rest)]  5.18 us
    ppermute x1, starting transfers between devices, shards(): other = lax.ppermute(rows, 'core', swap)  2.05 us
    ppermute x1, starting transfers between devices, shards(): far_points = lax.ppermute(near[0], NAMES, from_group((1, -1)))  1.91 us
  transfers between devices with their start and end apart: 4, of which 3 were waited for; matrix products, arithmetic and copies ran while one was open for 0% of the time, Pallas kernels for 9%

profile of v5, /device:TPU:14, one launch (start us, length us, event | category | flops | bytes accessed | tf_op | source)
XLA Modules:
  0.0 92.3 jit_solution(4282517906729665933)
XLA Ops:
  0.0 1.2 %shard_map.28 = (bf16[256,1024]{1,0:T(8,128)(2,1)S(1)}, bf16[256,1024]{1,0:T(8,128)(2,1)S(1)}) custom-call(s32[1]{0:T(128)} %bitcast.core, bf16[512,1024]{1,0:T(8,128)(2,1)} %points.1), custom_call_target="tpu_custom_call" | custom-call | tf_op jit(solution)/shard_map/pallas_call | solution.py:211
  1.2 0.0 copy-start
  1.2 2.1 %collective-permute-start = (bf16[1024,1024]{1,0:T(8,128)(2,1)}, bf16[1024,1024]{1,0:T(8,128)(2,1)S(1)}, u32[]{:S(2)}, u32[]{:S(2)}) collective-permute-start(bf16[1024,1024]{1,0:T(8,128)(2,1)} %d0.5), channel_id=1, source_target_pairs={{0,1},{1,0},{2,3},{3,2},{4,5},{5,4},{6,7},{7,6},{8,9},{9,8},{10,11... | collective-permute-start | bytes 6291464 | tf_op jit(solution)/shard_map/ppermute | solution.py:221
  3.3 2.7 %collective-permute-start.1 = (bf16[256,1024]{1,0:T(8,128)(2,1)S(1)}, bf16[256,1024]{1,0:T(8,128)(2,1)S(1)}, u32[]{:S(2)}, u32[]{:S(2)}) collective-permute-start(bf16[256,1024]{1,0:T(8,128)(2,1)S(1)} %get-tuple-element.19.mine), channel_id=1, source_target_pairs={{64,0},{193,1},{66,2},{195,3},{68,4},{197,5},{70,6},{199,7},{72,8}... | collective-permute-start | bytes 1572872 | tf_op jit(solution)/shard_map/ppermute | solution.py:219
  6.0 2.4 %collective-permute-start.2 = (bf16[256,1024]{1,0:T(8,128)(2,1)S(1)}, bf16[256,1024]{1,0:T(8,128)(2,1)S(1)}, u32[]{:S(2)}, u32[]{:S(2)}) collective-permute-start(bf16[256,1024]{1,0:T(8,128)(2,1)S(1)} %get-tuple-element.20.rest), channel_id=1, source_target_pairs={{64,0},{193,1},{66,2},{195,3},{68,4},{197,5},{70,6},{199,7},{72,8}... | collective-permute-start | bytes 1572872 | tf_op jit(solution)/shard_map/ppermute | solution.py:219
  8.5 0.0 collective-permute-done.rows.d1
  8.5 1.9 %shard_map.29 = (bf16[512,1024]{1,0:T(8,128)(2,1)S(1)}, f32[1,1024]{1,0:T(1,128)S(1)}) custom-call(bf16[256,1024]{1,0:T(8,128)(2,1)S(1)} %get-tuple-element.19.mine, bf16[256,1024]{1,0:T(8,128)(2,1)S(1)} %get-tuple-element.20.rest, bf16[1024,1024]{1,0:T(8,128)(2,1)S(1)} %collective-permute-done.rows.d1), custom_call_target="tpu_custom_call" | custom-call | flops 1073741824 | bytes 3145728 | tf_op jit(solution)/shard_map/pallas_call | solution.py:46
  10.4 0.0 copy-done
  10.4 2.4 %shard_map.30 = (bf16[512,1024]{1,0:T(8,128)(2,1)S(1)}, f32[1,1024]{1,0:T(1,128)S(1)}, f32[512,256]{1,0:T(8,128)S(1)}) custom-call(bf16[256,1024]{1,0:T(8,128)(2,1)S(1)} %get-tuple-element.19.mine, bf16[256,1024]{1,0:T(8,128)(2,1)S(1)} %get-tuple-element.20.rest, bf16[1024,1024]{1,0:T(8,128)(2,1)S(1)} %copy-done, bf16[512,1024]{1,0:T(8,128)(2,1)S(1)} %get-tuple-element.22.a1), custom_call_target="tpu_custom_call" | custom-call | flops 1610612736 | bytes 4194304 | tf_op jit(solution)/shard_map/pallas_call | solution.py:46
  12.8 3.7 %collective-permute-done.1.b = bf16[256,1024]{1,0:T(8,128)(2,1)S(1)} collective-permute-done((bf16[256,1024]{1,0:T(8,128)(2,1)S(1)}, bf16[256,1024]{1,0:T(8,128)(2,1)S(1)}, u32[]{:S(2)}, u32[]{:S(2)}) %collective-permute-start.1) | collective-permute-done | bytes 524320 | tf_op jit(solution)/shard_map/ppermute | solution.py:219
  16.5 1.9 %collective-permute-start.3 = (bf16[256,1024]{1,0:T(8,128)(2,1)S(1)}, bf16[256,1024]{1,0:T(8,128)(2,1)S(1)}, u32[]{:S(2)}, u32[]{:S(2)}) collective-permute-start(bf16[256,1024]{1,0:T(8,128)(2,1)S(1)} %collective-permute-done.1.b), channel_id=1, source_target_pairs={{64,0},{451,1},{66,2},{449,3},{68,4},{455,5},{70,6},{453,7},{72,8}... | collective-permute-start | bytes 1572872 | tf_op jit(solution)/shard_map/ppermute | solution.py:225
  18.4 2.0 %shard_map.31.near = f32[512,256]{1,0:T(8,128)S(1)} custom-call(bf16[256,1024]{1,0:T(8,128)(2,1)S(1)} %collective-permute-done.1.b, bf16[1024,1024]{1,0:T(8,128)(2,1)S(1)} %copy-done, bf16[1024,1024]{1,0:T(8,128)(2,1)S(1)} %collective-permute-done.rows.d1, f32[1,1024]{1,0:T(1,128)S(1)} %get-tuple-element.26.e0, f32[1,1024]{1,0:T(1,128)S(1)} %get-tuple-element.27.e1, ...), custom_call_target="tpu_custom_call" | custom-call | flops 1610612736 | bytes 6823936 | tf_op jit(solution)/shard_map/pallas_call | solution.py:46
  20.4 1.7 %collective-permute-done.2.b = bf16[256,1024]{1,0:T(8,128)(2,1)S(1)} collective-permute-done((bf16[256,1024]{1,0:T(8,128)(2,1)S(1)}, bf16[256,1024]{1,0:T(8,128)(2,1)S(1)}, u32[]{:S(2)}, u32[]{:S(2)}) %collective-permute-start.2) | collective-permute-done | bytes 524320 | tf_op jit(solution)/shard_map/ppermute | solution.py:219
  22.1 2.0 %shard_map.32.rest = f32[512,256]{1,0:T(8,128)S(1)} custom-call(bf16[256,1024]{1,0:T(8,128)(2,1)S(1)} %collective-permute-done.2.b, bf16[1024,1024]{1,0:T(8,128)(2,1)S(1)} %copy-done, bf16[1024,1024]{1,0:T(8,128)(2,1)S(1)} %collective-permute-done.rows.d1, f32[1,1024]{1,0:T(1,128)S(1)} %get-tuple-element.26.e0, f32[1,1024]{1,0:T(1,128)S(1)} %get-tuple-element.27.e1, ...), custom_call_target="tpu_custom_call" | custom-call | flops 1610612736 | bytes 6823936 | tf_op jit(solution)/shard_map/pallas_call | solution.py:46
  24.1 5.5 %collective-permute-done.3.b = bf16[256,1024]{1,0:T(8,128)(2,1)S(1)} collective-permute-done((bf16[256,1024]{1,0:T(8,128)(2,1)S(1)}, bf16[256,1024]{1,0:T(8,128)(2,1)S(1)}, u32[]{:S(2)}, u32[]{:S(2)}) %collective-permute-start.3) | collective-permute-done | bytes 524320 | tf_op jit(solution)/shard_map/ppermute | solution.py:225
  29.7 2.6 %shard_map.33 = bf16[512,1024]{1,0:T(8,128)(2,1)S(1)} custom-call(s32[1]{0:T(128)} %bitcast.core, f32[512,256]{1,0:T(8,128)S(1)} %get-tuple-element.23.g0, f32[512,256]{1,0:T(8,128)S(1)} %shard_map.31.near, f32[512,256]{1,0:T(8,128)S(1)} %shard_map.32.rest, bf16[512,1024]{1,0:T(8,128)(2,1)S(1)} %get-tuple-element.28.a0, ...), custom_call_target="tpu_custom_call" | custom-call | flops 1610612736 | bytes 8396804 | tf_op jit(solution)/shard_map/pallas_call | solution.py:46
  32.2 23.2 %all_to_all.16 = bf16[8,64,1024]{2,1,0:T(8,128)(2,1)S(1)} all-to-all(bf16[8,64,1024]{2,1,0:T(8,128)(2,1)S(1)} %bitcast.5), channel_id=1, replica_groups=mesh['y_lo'=2,'x'=4,'z_hi'=8,'z_lo'=2,'y_hi'=2,'core'=2] {'z_lo','y_hi',..., dimensions={0} | all-to-all | bytes 2097152 | tf_op jit(solution)/shard_map/all_to_all | solution.py:233
  55.5 0.8 shard_map.34
  56.3 35.2 %all_to_all.17.chunks = bf16[8,8,2048]{2,1,0:T(8,128)(2,1)S(1)} all-to-all(bf16[8,8,2048]{2,1,0:T(8,128)(2,1)S(1)} %bitcast.6), channel_id=1, replica_groups=mesh['y_lo'=2,'x'=4,'z_hi'=8,'z_lo'=2,'y_hi'=2,'core'=2] {'z_hi'}, dimensions={0} | all-to-all | bytes 524288 | tf_op jit(solution)/shard_map/all_to_all | solution.py:235
  91.5 0.8 shard_map.35
Async XLA Ops:
  1.2 9.2 %copy-start = (bf16[1024,1024]{1,0:T(8,128)(2,1)S(1)}, bf16[1024,1024]{1,0:T(8,128)(2,1)}, u32[]{:S(2)}) copy-start(bf16[1024,1024]{1,0:T(8,128)(2,1)} %d0.5) | copy-start | bytes 6291460
  1.2 7.3 %collective-permute-start = (bf16[1024,1024]{1,0:T(8,128)(2,1)}, bf16[1024,1024]{1,0:T(8,128)(2,1)S(1)}, u32[]{:S(2)}, u32[]{:S(2)}) collective-permute-start(bf16[1024,1024]{1,0:T(8,128)(2,1)} %d0.5), channel_id=1, source_target_pairs={{0,1},{1,0},{2,3},{3,2},{4,5},{5,4},{6,7},{7,6},{8,9},{9,8},{10,11... | collective-permute-start | bytes 6291464 | tf_op jit(solution)/shard_map/ppermute | solution.py:221
  3.3 13.2 %collective-permute-start.1 = (bf16[256,1024]{1,0:T(8,128)(2,1)S(1)}, bf16[256,1024]{1,0:T(8,128)(2,1)S(1)}, u32[]{:S(2)}, u32[]{:S(2)}) collective-permute-start(bf16[256,1024]{1,0:T(8,128)(2,1)S(1)} %get-tuple-element.19.mine), channel_id=1, source_target_pairs={{64,0},{193,1},{66,2},{195,3},{68,4},{197,5},{70,6},{199,7},{72,8}... | collective-permute-start | bytes 1572872 | tf_op jit(solution)/shard_map/ppermute | solution.py:219
  6.0 16.1 %collective-permute-start.2 = (bf16[256,1024]{1,0:T(8,128)(2,1)S(1)}, bf16[256,1024]{1,0:T(8,128)(2,1)S(1)}, u32[]{:S(2)}, u32[]{:S(2)}) collective-permute-start(bf16[256,1024]{1,0:T(8,128)(2,1)S(1)} %get-tuple-element.20.rest), channel_id=1, source_target_pairs={{64,0},{193,1},{66,2},{195,3},{68,4},{197,5},{70,6},{199,7},{72,8}... | collective-permute-start | bytes 1572872 | tf_op jit(solution)/shard_map/ppermute | solution.py:219
  16.5 13.2 %collective-permute-start.3 = (bf16[256,1024]{1,0:T(8,128)(2,1)S(1)}, bf16[256,1024]{1,0:T(8,128)(2,1)S(1)}, u32[]{:S(2)}, u32[]{:S(2)}) collective-permute-start(bf16[256,1024]{1,0:T(8,128)(2,1)S(1)} %collective-permute-done.1.b), channel_id=1, source_target_pairs={{64,0},{451,1},{66,2},{449,3},{68,4},{455,5},{70,6},{453,7},{72,8}... | collective-permute-start | bytes 1572872 | tf_op jit(solution)/shard_map/ppermute | solution.py:225

commit v6 on v5

--- a/solution.py
+++ b/solution.py
@@ -95,8 +95,8 @@
 
 
 def fill(points, inv, rows, rows_inv, out):
-    for i in range(ENV // 256):
-        part = slice(i * 256, (i + 1) * 256)
+    for i in range(ENV // 512):
+        part = slice(i * 512, (i + 1) * 512)
         out[:, part] = powered(nt(points[...], rows[part, :]), inv, rows_inv[:, part])
 
 
@@ -220,9 +220,9 @@
     mine, rest, rows = lax.optimization_barrier((mine, rest, descriptors))
     other = lax.ppermute(rows, "core", swap)
     a1, e1 = call(own_kernel, (one, line), (mine, rest, other), flops=work)
+    near[0], e1 = lax.optimization_barrier((near[0], e1))
+    far_points = lax.ppermute(near[0], NAMES, from_group((1, -1)))
     a0, e0, g_aa = call(second_kernel, (one, line, gram), (mine, rest, descriptors, a1), flops=work * 3 // 2)
-    near[0], e0 = lax.optimization_barrier((near[0], e0))
-    far_points = lax.ppermute(near[0], NAMES, from_group((1, -1)))
     tiles = []
     for points in near:
         inputs = (points, descriptors, other, e0, e1, a0, a1)

time: 92.6 us -> 92.6 us (level)
  transfers between devices with their start and end apart: 4 -> 4, of which waited for: 3 -> 2; matrix products, arithmetic and copies ran while one was open for 0% -> 0% of each run, Pallas kernels for 9% -> 9%
where the time goes in v6:
time: 92.6 us; the launch traced here: 92.3 us
  blocking collectives  58.4 us (63%)
  Pallas kernels  13.8 us (15%)
  waiting for transfers between devices  10.8 us (12%)
  starting transfers between devices  9.14 us (10%)
    all_to_all x1, blocking collectives, shards(): got = lax.all_to_all(sent.reshape(8, 8, 2 * WIDE), 'z_hi', 0, 0, tiled=True)  35.2 us
    all_to_all x1, blocking collectives, shards(): got = lax.all_to_all(sent, ('z_lo', 'y_hi', 'core'), 0, 0, tiled=True)  23.2 us
    pallas_call x7, Pallas kernels, call(): pl.pallas_call(body, out_shape=outs, in_specs=[pl.BlockSpec(memory_space=...  12.6 us
    ppermute x2, waiting for transfers between devices, shards(): near = [lax.ppermute(v, NAMES, from_group((1, 3))) for v in (mine, rest)]  6.02 us
    ppermute x2, starting transfers between devices, shards(): near = [lax.ppermute(v, NAMES, from_group((1, 3))) for v in (mine, rest)]  5.18 us
    ppermute x1, waiting for transfers between devices, shards(): far_points = lax.ppermute(near[0], NAMES, from_group((1, -1)))  4.76 us
    ppermute x1, starting transfers between devices, shards(): other = lax.ppermute(rows, 'core', swap)  2.05 us
    ppermute x1, starting transfers between devices, shards(): far_points = lax.ppermute(near[0], NAMES, from_group((1, -1)))  1.91 us
  transfers between devices with their start and end apart: 4, of which 2 were waited for; matrix products, arithmetic and copies ran while one was open for 0% of the time, Pallas kernels for 9%

profile of v6, /device:TPU:14, one launch (start us, length us, event | category | flops | bytes accessed | tf_op | source)
XLA Modules:
  0.0 92.3 jit_solution(7519030647816363164)
XLA Ops:
  0.0 1.2 %shard_map.28 = (bf16[256,1024]{1,0:T(8,128)(2,1)S(1)}, bf16[256,1024]{1,0:T(8,128)(2,1)S(1)}) custom-call(s32[1]{0:T(128)} %bitcast.core, bf16[512,1024]{1,0:T(8,128)(2,1)} %points.1), custom_call_target="tpu_custom_call" | custom-call | tf_op jit(solution)/shard_map/pallas_call | solution.py:211
  1.2 0.0 copy-start
  1.2 2.1 %collective-permute-start = (bf16[1024,1024]{1,0:T(8,128)(2,1)}, bf16[1024,1024]{1,0:T(8,128)(2,1)S(1)}, u32[]{:S(2)}, u32[]{:S(2)}) collective-permute-start(bf16[1024,1024]{1,0:T(8,128)(2,1)} %d0.5), channel_id=1, source_target_pairs={{0,1},{1,0},{2,3},{3,2},{4,5},{5,4},{6,7},{7,6},{8,9},{9,8},{10,11... | collective-permute-start | bytes 6291464 | tf_op jit(solution)/shard_map/ppermute | solution.py:221
  3.3 2.7 %collective-permute-start.1 = (bf16[256,1024]{1,0:T(8,128)(2,1)S(1)}, bf16[256,1024]{1,0:T(8,128)(2,1)S(1)}, u32[]{:S(2)}, u32[]{:S(2)}) collective-permute-start(bf16[256,1024]{1,0:T(8,128)(2,1)S(1)} %get-tuple-element.19.mine), channel_id=1, source_target_pairs={{64,0},{193,1},{66,2},{195,3},{68,4},{197,5},{70,6},{199,7},{72,8}... | collective-permute-start | bytes 1572872 | tf_op jit(solution)/shard_map/ppermute | solution.py:219
  6.0 2.4 %collective-permute-start.2 = (bf16[256,1024]{1,0:T(8,128)(2,1)S(1)}, bf16[256,1024]{1,0:T(8,128)(2,1)S(1)}, u32[]{:S(2)}, u32[]{:S(2)}) collective-permute-start(bf16[256,1024]{1,0:T(8,128)(2,1)S(1)} %get-tuple-element.20.rest), channel_id=1, source_target_pairs={{64,0},{193,1},{66,2},{195,3},{68,4},{197,5},{70,6},{199,7},{72,8}... | collective-permute-start | bytes 1572872 | tf_op jit(solution)/shard_map/ppermute | solution.py:219
  8.5 0.0 collective-permute-done.rows.d1
  8.5 2.0 %shard_map.29 = (bf16[512,1024]{1,0:T(8,128)(2,1)S(1)}, f32[1,1024]{1,0:T(1,128)S(1)}) custom-call(bf16[256,1024]{1,0:T(8,128)(2,1)S(1)} %get-tuple-element.19.mine, bf16[256,1024]{1,0:T(8,128)(2,1)S(1)} %get-tuple-element.20.rest, bf16[1024,1024]{1,0:T(8,128)(2,1)S(1)} %collective-permute-done.rows.d1), custom_call_target="tpu_custom_call" | custom-call | flops 1073741824 | bytes 3145728 | tf_op jit(solution)/shard_map/pallas_call | solution.py:46
  10.5 6.0 %collective-permute-done.1.b = bf16[256,1024]{1,0:T(8,128)(2,1)S(1)} collective-permute-done((bf16[256,1024]{1,0:T(8,128)(2,1)S(1)}, bf16[256,1024]{1,0:T(8,128)(2,1)S(1)}, u32[]{:S(2)}, u32[]{:S(2)}) %collective-permute-start.1) | collective-permute-done | bytes 524320 | tf_op jit(solution)/shard_map/ppermute | solution.py:219
  16.5 1.9 %collective-permute-start.3 = (bf16[256,1024]{1,0:T(8,128)(2,1)S(1)}, bf16[256,1024]{1,0:T(8,128)(2,1)S(1)}, u32[]{:S(2)}, u32[]{:S(2)}) collective-permute-start(bf16[256,1024]{1,0:T(8,128)(2,1)S(1)} %collective-permute-done.1.b), channel_id=1, source_target_pairs={{64,0},{451,1},{66,2},{449,3},{68,4},{455,5},{70,6},{453,7},{72,8}... | collective-permute-start | bytes 1572872 | tf_op jit(solution)/shard_map/ppermute | solution.py:224
  18.4 0.0 copy-done
  18.4 2.4 %shard_map.30 = (bf16[512,1024]{1,0:T(8,128)(2,1)S(1)}, f32[1,1024]{1,0:T(1,128)S(1)}, f32[512,256]{1,0:T(8,128)S(1)}) custom-call(bf16[256,1024]{1,0:T(8,128)(2,1)S(1)} %get-tuple-element.19.mine, bf16[256,1024]{1,0:T(8,128)(2,1)S(1)} %get-tuple-element.20.rest, bf16[1024,1024]{1,0:T(8,128)(2,1)S(1)} %copy-done, bf16[512,1024]{1,0:T(8,128)(2,1)S(1)} %get-tuple-element.22.a1), custom_call_target="tpu_custom_call" | custom-call | flops 1610612736 | bytes 4194304 | tf_op jit(solution)/shard_map/pallas_call | solution.py:46
  20.8 2.0 %shard_map.31.near = f32[512,256]{1,0:T(8,128)S(1)} custom-call(bf16[256,1024]{1,0:T(8,128)(2,1)S(1)} %collective-permute-done.1.b, bf16[1024,1024]{1,0:T(8,128)(2,1)S(1)} %copy-done, bf16[1024,1024]{1,0:T(8,128)(2,1)S(1)} %collective-permute-done.rows.d1, f32[1,1024]{1,0:T(1,128)S(1)} %get-tuple-element.26.e0, f32[1,1024]{1,0:T(1,128)S(1)} %get-tuple-element.27.e1, ...), custom_call_target="tpu_custom_call" | custom-call | flops 1610612736 | bytes 6823936 | tf_op jit(solution)/shard_map/pallas_call | solution.py:46
  22.9 0.0 collective-permute-done.2.b
  22.9 2.0 %shard_map.32.rest = f32[512,256]{1,0:T(8,128)S(1)} custom-call(bf16[256,1024]{1,0:T(8,128)(2,1)S(1)} %collective-permute-done.2.b, bf16[1024,1024]{1,0:T(8,128)(2,1)S(1)} %copy-done, bf16[1024,1024]{1,0:T(8,128)(2,1)S(1)} %collective-permute-done.rows.d1, f32[1,1024]{1,0:T(1,128)S(1)} %get-tuple-element.26.e0, f32[1,1024]{1,0:T(1,128)S(1)} %get-tuple-element.27.e1, ...), custom_call_target="tpu_custom_call" | custom-call | flops 1610612736 | bytes 6823936 | tf_op jit(solution)/shard_map/pallas_call | solution.py:46
  24.9 4.8 %collective-permute-done.3.b = bf16[256,1024]{1,0:T(8,128)(2,1)S(1)} collective-permute-done((bf16[256,1024]{1,0:T(8,128)(2,1)S(1)}, bf16[256,1024]{1,0:T(8,128)(2,1)S(1)}, u32[]{:S(2)}, u32[]{:S(2)}) %collective-permute-start.3) | collective-permute-done | bytes 524320 | tf_op jit(solution)/shard_map/ppermute | solution.py:224
  29.7 2.6 %shard_map.33 = bf16[512,1024]{1,0:T(8,128)(2,1)S(1)} custom-call(s32[1]{0:T(128)} %bitcast.core, f32[512,256]{1,0:T(8,128)S(1)} %get-tuple-element.23.g0, f32[512,256]{1,0:T(8,128)S(1)} %shard_map.31.near, f32[512,256]{1,0:T(8,128)S(1)} %shard_map.32.rest, bf16[512,1024]{1,0:T(8,128)(2,1)S(1)} %get-tuple-element.28.a0, ...), custom_call_target="tpu_custom_call" | custom-call | flops 1610612736 | bytes 8396804 | tf_op jit(solution)/shard_map/pallas_call | solution.py:46
  32.3 23.2 %all_to_all.16 = bf16[8,64,1024]{2,1,0:T(8,128)(2,1)S(1)} all-to-all(bf16[8,64,1024]{2,1,0:T(8,128)(2,1)S(1)} %bitcast.5), channel_id=1, replica_groups=mesh['y_lo'=2,'x'=4,'z_hi'=8,'z_lo'=2,'y_hi'=2,'core'=2] {'z_lo','y_hi',..., dimensions={0} | all-to-all | bytes 2097152 | tf_op jit(solution)/shard_map/all_to_all | solution.py:233
  55.5 0.8 shard_map.34
  56.3 35.2 %all_to_all.17.chunks = bf16[8,8,2048]{2,1,0:T(8,128)(2,1)S(1)} all-to-all(bf16[8,8,2048]{2,1,0:T(8,128)(2,1)S(1)} %bitcast.6), channel_id=1, replica_groups=mesh['y_lo'=2,'x'=4,'z_hi'=8,'z_lo'=2,'y_hi'=2,'core'=2] {'z_hi'}, dimensions={0} | all-to-all | bytes 524288 | tf_op jit(solution)/shard_map/all_to_all | solution.py:235
  91.5 0.8 shard_map.35
Async XLA Ops:
  1.2 17.2 %copy-start = (bf16[1024,1024]{1,0:T(8,128)(2,1)S(1)}, bf16[1024,1024]{1,0:T(8,128)(2,1)}, u32[]{:S(2)}) copy-start(bf16[1024,1024]{1,0:T(8,128)(2,1)} %d0.5) | copy-start | bytes 6291460
  1.2 7.3 %collective-permute-start = (bf16[1024,1024]{1,0:T(8,128)(2,1)}, bf16[1024,1024]{1,0:T(8,128)(2,1)S(1)}, u32[]{:S(2)}, u32[]{:S(2)}) collective-permute-start(bf16[1024,1024]{1,0:T(8,128)(2,1)} %d0.5), channel_id=1, source_target_pairs={{0,1},{1,0},{2,3},{3,2},{4,5},{5,4},{6,7},{7,6},{8,9},{9,8},{10,11... | collective-permute-start | bytes 6291464 | tf_op jit(solution)/shard_map/ppermute | solution.py:221
  3.3 13.2 %collective-permute-start.1 = (bf16[256,1024]{1,0:T(8,128)(2,1)S(1)}, bf16[256,1024]{1,0:T(8,128)(2,1)S(1)}, u32[]{:S(2)}, u32[]{:S(2)}) collective-permute-start(bf16[256,1024]{1,0:T(8,128)(2,1)S(1)} %get-tuple-element.19.mine), channel_id=1, source_target_pairs={{64,0},{193,1},{66,2},{195,3},{68,4},{197,5},{70,6},{199,7},{72,8}... | collective-permute-start | bytes 1572872 | tf_op jit(solution)/shard_map/ppermute | solution.py:219
  6.0 16.8 %collective-permute-start.2 = (bf16[256,1024]{1,0:T(8,128)(2,1)S(1)}, bf16[256,1024]{1,0:T(8,128)(2,1)S(1)}, u32[]{:S(2)}, u32[]{:S(2)}) collective-permute-start(bf16[256,1024]{1,0:T(8,128)(2,1)S(1)} %get-tuple-element.20.rest), channel_id=1, source_target_pairs={{64,0},{193,1},{66,2},{195,3},{68,4},{197,5},{70,6},{199,7},{72,8}... | collective-permute-start | bytes 1572872 | tf_op jit(solution)/shard_map/ppermute | solution.py:219
  16.5 13.2 %collective-permute-start.3 = (bf16[256,1024]{1,0:T(8,128)(2,1)S(1)}, bf16[256,1024]{1,0:T(8,128)(2,1)S(1)}, u32[]{:S(2)}, u32[]{:S(2)}) collective-permute-start(bf16[256,1024]{1,0:T(8,128)(2,1)S(1)} %collective-permute-done.1.b), channel_id=1, source_target_pairs={{64,0},{451,1},{66,2},{449,3},{68,4},{455,5},{70,6},{453,7},{72,8}... | collective-permute-start | bytes 1572872 | tf_op jit(solution)/shard_map/ppermute | solution.py:224

commit v7 on v6

--- a/solution.py
+++ b/solution.py
@@ -69,15 +69,11 @@
     return (KERNEL_VARIANCE * (square * square)).astype(jnp.bfloat16)
 
 
-def halves_kernel(core, points, out, rest, sems):
-    copies = []
-    for i, (half, to) in enumerate(((core[0], out), (1 - core[0], rest))):
-        rows = pl.ds(pl.multiple_of(half * HALF, HALF), HALF)
-        copies.append(pltpu.make_async_copy(points.at[rows, :], to, sems.at[i]))
-    for copy in copies:
-        copy.start()
-    for copy in copies:
-        copy.wait()
+def half_kernel(half, points, out, sem):
+    rows = pl.ds(pl.multiple_of(half[0] * HALF, HALF), HALF)
+    copy = pltpu.make_async_copy(points.at[rows, :], out, sem)
+    copy.start()
+    copy.wait()
 
 
 def own_kernel(mine, rest, rows, out, rows_inv):
@@ -208,16 +204,19 @@
     far = pl.BlockSpec(memory_space=pltpu.HBM)
     points_far = pltpu.with_memory_space_constraint(sparse_points, pltpu.HBM)
     whole = pl.BlockSpec(memory_space=pltpu.VMEM)
-    mine, rest = pl.pallas_call(
-        halves_kernel,
-        out_shape=(jax.ShapeDtypeStruct((HALF, D), bf16), jax.ShapeDtypeStruct((HALF, D), bf16)),
-        in_specs=[pl.BlockSpec(memory_space=pltpu.SMEM), far],
-        out_specs=(whole, whole),
-        scratch_shapes=[pltpu.SemaphoreType.DMA((2,))],
-        compiler_params=pltpu.CompilerParams(vmem_limit_bytes=VMEM),
-    )(number, points_far)
+    mine, rest = (
+        pl.pallas_call(
+            half_kernel,
+            out_shape=jax.ShapeDtypeStruct((HALF, D), bf16),
+            in_specs=[pl.BlockSpec(memory_space=pltpu.SMEM), far],
+            out_specs=whole,
+            scratch_shapes=[pltpu.SemaphoreType.DMA],
+            compiler_params=pltpu.CompilerParams(vmem_limit_bytes=VMEM),
+        )(i, points_far)
+        for i in (number, 1 - number)
+    )
     near = [lax.ppermute(v, NAMES, from_group((1, 3))) for v in (mine, rest)]
-    mine, rest, rows = lax.optimization_barrier((mine, rest, descriptors))
+    mine, rows = lax.optimization_barrier((mine, descriptors))
     other = lax.ppermute(rows, "core", swap)
     a1, e1 = call(own_kernel, (one, line), (mine, rest, other), flops=work)
     near[0], e1 = lax.optimization_barrier((near[0], e1))

time: 92.6 us -> 92.4 us (level)
  waiting for transfers between devices: 10.8 us -> 9.7 us
    ppermute x2, waiting for transfers between devices: 6.02 us -> 4.86 us  [shards(): near = [lax.ppermute(v, NAMES, from_group((1, 3))) for v in (mine, rest)]]
    pallas_call x1 -> x2, Pallas kernels: 1.22 us -> 2.1 us  [shards(): pl.pallas_call(half_kernel, out_shape=jax.ShapeDtypeStruct((HALF, D), bf1...]
  transfers between devices with their start and end apart: 4 -> 4, of which waited for: 2 -> 2; matrix products, arithmetic and copies ran while one was open for 0% -> 0% of each run, Pallas kernels for 9% -> 10%
where the time goes in v7:
time: 92.4 us; the launch traced here: 92 us
  blocking collectives  58.4 us (63%)
  Pallas kernels  14.6 us (16%)
  waiting for transfers between devices  9.7 us (10%)
  starting transfers between devices  9.14 us (10%)
    all_to_all x1, blocking collectives, shards(): got = lax.all_to_all(sent.reshape(8, 8, 2 * WIDE), 'z_hi', 0, 0, tiled=True)  35.2 us
    all_to_all x1, blocking collectives, shards(): got = lax.all_to_all(sent, ('z_lo', 'y_hi', 'core'), 0, 0, tiled=True)  23.2 us
    pallas_call x7, Pallas kernels, call(): pl.pallas_call(body, out_shape=outs, in_specs=[pl.BlockSpec(memory_space=...  12.5 us
    ppermute x2, starting transfers between devices, shards(): near = [lax.ppermute(v, NAMES, from_group((1, 3))) for v in (mine, rest)]  5.31 us
    ppermute x2, waiting for transfers between devices, shards(): near = [lax.ppermute(v, NAMES, from_group((1, 3))) for v in (mine, rest)]  4.86 us
    ppermute x1, waiting for transfers between devices, shards(): far_points = lax.ppermute(near[0], NAMES, from_group((1, -1)))  4.83 us
    pallas_call x2, Pallas kernels, shards(): pl.pallas_call(half_kernel, out_shape=jax.ShapeDtypeStruct((HALF, D), bf1...  2.1 us
    ppermute x1, starting transfers between devices, shards(): other = lax.ppermute(rows, 'core', swap)  1.92 us
  transfers between devices with their start and end apart: 4, of which 2 were waited for; matrix products, arithmetic and copies ran while one was open for 0% of the time, Pallas kernels for 10%

profile of v7, /device:TPU:14, one launch (start us, length us, event | category | flops | bytes accessed | tf_op | source)
XLA Modules:
  0.0 92.0 jit_solution(18261159367167921146)
XLA Ops:
  0.0 1.0 %shard_map.28.mine = bf16[256,1024]{1,0:T(8,128)(2,1)S(1)} custom-call(s32[1]{0:T(128)} %bitcast.half.core, bf16[512,1024]{1,0:T(8,128)(2,1)} %points.3), custom_call_target="tpu_custom_call" | custom-call | tf_op jit(solution)/shard_map/pallas_call | solution.py:208
  1.1 1.9 %collective-permute-start = (bf16[1024,1024]{1,0:T(8,128)(2,1)}, bf16[1024,1024]{1,0:T(8,128)(2,1)S(1)}, u32[]{:S(2)}, u32[]{:S(2)}) collective-permute-start(bf16[1024,1024]{1,0:T(8,128)(2,1)} %d0.5), channel_id=1, source_target_pairs={{0,1},{1,0},{2,3},{3,2},{4,5},{5,4},{6,7},{7,6},{8,9},{9,8},{10,11... | collective-permute-start | bytes 6291464 | tf_op jit(solution)/shard_map/ppermute | solution.py:220
  3.0 2.7 %collective-permute-start.1 = (bf16[256,1024]{1,0:T(8,128)(2,1)S(1)}, bf16[256,1024]{1,0:T(8,128)(2,1)S(1)}, u32[]{:S(2)}, u32[]{:S(2)}) collective-permute-start(bf16[256,1024]{1,0:T(8,128)(2,1)S(1)} %shard_map.28.mine), channel_id=1, source_target_pairs={{64,0},{193,1},{66,2},{195,3},{68,4},{197,5},{70,6},{199,7},{72,8}... | collective-permute-start | bytes 1572872 | tf_op jit(solution)/shard_map/ppermute | solution.py:218
  5.7 1.1 %shard_map.29.rest = bf16[256,1024]{1,0:T(8,128)(2,1)S(1)} custom-call(s32[1]{0:T(128)S(6)} %sub.3.half, bf16[512,1024]{1,0:T(8,128)(2,1)} %points.3), custom_call_target="tpu_custom_call" | custom-call | tf_op jit(solution)/shard_map/pallas_call | solution.py:208
  6.8 0.0 copy-start
  6.8 2.6 %collective-permute-start.2 = (bf16[256,1024]{1,0:T(8,128)(2,1)S(1)}, bf16[256,1024]{1,0:T(8,128)(2,1)S(1)}, u32[]{:S(2)}, u32[]{:S(2)}) collective-permute-start(bf16[256,1024]{1,0:T(8,128)(2,1)S(1)} %shard_map.29.rest), channel_id=1, source_target_pairs={{64,0},{193,1},{66,2},{195,3},{68,4},{197,5},{70,6},{199,7},{72,8}... | collective-permute-start | bytes 1572872 | tf_op jit(solution)/shard_map/ppermute | solution.py:218
  9.4 0.0 collective-permute-done.rows.d1
  9.4 1.9 %shard_map.30 = (bf16[512,1024]{1,0:T(8,128)(2,1)S(1)}, f32[1,1024]{1,0:T(1,128)S(1)}) custom-call(bf16[256,1024]{1,0:T(8,128)(2,1)S(1)} %shard_map.28.mine, bf16[256,1024]{1,0:T(8,128)(2,1)S(1)} %shard_map.29.rest, bf16[1024,1024]{1,0:T(8,128)(2,1)S(1)} %collective-permute-done.rows.d1), custom_call_target="tpu_custom_call" | custom-call | flops 1073741824 | bytes 3145728 | tf_op jit(solution)/shard_map/pallas_call | solution.py:46
  11.3 4.9 %collective-permute-done.1.b = bf16[256,1024]{1,0:T(8,128)(2,1)S(1)} collective-permute-done((bf16[256,1024]{1,0:T(8,128)(2,1)S(1)}, bf16[256,1024]{1,0:T(8,128)(2,1)S(1)}, u32[]{:S(2)}, u32[]{:S(2)}) %collective-permute-start.1) | collective-permute-done | bytes 524320 | tf_op jit(solution)/shard_map/ppermute | solution.py:218
  16.2 1.9 %collective-permute-start.3 = (bf16[256,1024]{1,0:T(8,128)(2,1)S(1)}, bf16[256,1024]{1,0:T(8,128)(2,1)S(1)}, u32[]{:S(2)}, u32[]{:S(2)}) collective-permute-start(bf16[256,1024]{1,0:T(8,128)(2,1)S(1)} %collective-permute-done.1.b), channel_id=1, source_target_pairs={{64,0},{451,1},{66,2},{449,3},{68,4},{455,5},{70,6},{453,7},{72,8}... | collective-permute-start | bytes 1572872 | tf_op jit(solution)/shard_map/ppermute | solution.py:223
  18.1 0.0 copy-done
  18.1 2.4 %shard_map.31 = (bf16[512,1024]{1,0:T(8,128)(2,1)S(1)}, f32[1,1024]{1,0:T(1,128)S(1)}, f32[512,256]{1,0:T(8,128)S(1)}) custom-call(bf16[256,1024]{1,0:T(8,128)(2,1)S(1)} %shard_map.28.mine, bf16[256,1024]{1,0:T(8,128)(2,1)S(1)} %shard_map.29.rest, bf16[1024,1024]{1,0:T(8,128)(2,1)S(1)} %copy-done, bf16[512,1024]{1,0:T(8,128)(2,1)S(1)} %get-tuple-element.16.a1), custom_call_target="tpu_custom_call" | custom-call | flops 1610612736 | bytes 4194304 | tf_op jit(solution)/shard_map/pallas_call | solution.py:46
  20.5 2.0 %shard_map.32.near = f32[512,256]{1,0:T(8,128)S(1)} custom-call(bf16[256,1024]{1,0:T(8,128)(2,1)S(1)} %collective-permute-done.1.b, bf16[1024,1024]{1,0:T(8,128)(2,1)S(1)} %copy-done, bf16[1024,1024]{1,0:T(8,128)(2,1)S(1)} %collective-permute-done.rows.d1, f32[1,1024]{1,0:T(1,128)S(1)} %get-tuple-element.20.e0, f32[1,1024]{1,0:T(1,128)S(1)} %get-tuple-element.21.e1, ...), custom_call_target="tpu_custom_call" | custom-call | flops 1610612736 | bytes 6823936 | tf_op jit(solution)/shard_map/pallas_call | solution.py:46
  22.5 0.0 collective-permute-done.2.b
  22.5 2.0 %shard_map.33.rest = f32[512,256]{1,0:T(8,128)S(1)} custom-call(bf16[256,1024]{1,0:T(8,128)(2,1)S(1)} %collective-permute-done.2.b, bf16[1024,1024]{1,0:T(8,128)(2,1)S(1)} %copy-done, bf16[1024,1024]{1,0:T(8,128)(2,1)S(1)} %collective-permute-done.rows.d1, f32[1,1024]{1,0:T(1,128)S(1)} %get-tuple-element.20.e0, f32[1,1024]{1,0:T(1,128)S(1)} %get-tuple-element.21.e1, ...), custom_call_target="tpu_custom_call" | custom-call | flops 1610612736 | bytes 6823936 | tf_op jit(solution)/shard_map/pallas_call | solution.py:46
  24.5 4.8 %collective-permute-done.3.b = bf16[256,1024]{1,0:T(8,128)(2,1)S(1)} collective-permute-done((bf16[256,1024]{1,0:T(8,128)(2,1)S(1)}, bf16[256,1024]{1,0:T(8,128)(2,1)S(1)}, u32[]{:S(2)}, u32[]{:S(2)}) %collective-permute-start.3) | collective-permute-done | bytes 524320 | tf_op jit(solution)/shard_map/ppermute | solution.py:223
  29.3 2.6 %shard_map.34 = bf16[512,1024]{1,0:T(8,128)(2,1)S(1)} custom-call(s32[1]{0:T(128)} %bitcast.half.core, f32[512,256]{1,0:T(8,128)S(1)} %get-tuple-element.17.g0, f32[512,256]{1,0:T(8,128)S(1)} %shard_map.32.near, f32[512,256]{1,0:T(8,128)S(1)} %shard_map.33.rest, bf16[512,1024]{1,0:T(8,128)(2,1)S(1)} %get-tuple-element.22.a0, ...), custom_call_target="tpu_custom_call" | custom-call | flops 1610612736 | bytes 8396804 | tf_op jit(solution)/shard_map/pallas_call | solution.py:46
  31.9 23.2 %all_to_all.16 = bf16[8,64,1024]{2,1,0:T(8,128)(2,1)S(1)} all-to-all(bf16[8,64,1024]{2,1,0:T(8,128)(2,1)S(1)} %bitcast.5), channel_id=1, replica_groups=mesh['y_lo'=2,'x'=4,'z_hi'=8,'z_lo'=2,'y_hi'=2,'core'=2] {'z_lo','y_hi',..., dimensions={0} | all-to-all | bytes 2097152 | tf_op jit(solution)/shard_map/all_to_all | solution.py:232
  55.2 0.8 shard_map.35
  56.0 35.2 %all_to_all.17.chunks = bf16[8,8,2048]{2,1,0:T(8,128)(2,1)S(1)} all-to-all(bf16[8,8,2048]{2,1,0:T(8,128)(2,1)S(1)} %bitcast.6), channel_id=1, replica_groups=mesh['y_lo'=2,'x'=4,'z_hi'=8,'z_lo'=2,'y_hi'=2,'core'=2] {'z_hi'}, dimensions={0} | all-to-all | bytes 524288 | tf_op jit(solution)/shard_map/all_to_all | solution.py:234
  91.2 0.8 shard_map.36
Async XLA Ops:
  1.1 8.3 %collective-permute-start = (bf16[1024,1024]{1,0:T(8,128)(2,1)}, bf16[1024,1024]{1,0:T(8,128)(2,1)S(1)}, u32[]{:S(2)}, u32[]{:S(2)}) collective-permute-start(bf16[1024,1024]{1,0:T(8,128)(2,1)} %d0.5), channel_id=1, source_target_pairs={{0,1},{1,0},{2,3},{3,2},{4,5},{5,4},{6,7},{7,6},{8,9},{9,8},{10,11... | collective-permute-start | bytes 6291464 | tf_op jit(solution)/shard_map/ppermute | solution.py:220
  3.0 13.2 %collective-permute-start.1 = (bf16[256,1024]{1,0:T(8,128)(2,1)S(1)}, bf16[256,1024]{1,0:T(8,128)(2,1)S(1)}, u32[]{:S(2)}, u32[]{:S(2)}) collective-permute-start(bf16[256,1024]{1,0:T(8,128)(2,1)S(1)} %shard_map.28.mine), channel_id=1, source_target_pairs={{64,0},{193,1},{66,2},{195,3},{68,4},{197,5},{70,6},{199,7},{72,8}... | collective-permute-start | bytes 1572872 | tf_op jit(solution)/shard_map/ppermute | solution.py:218
  6.8 11.3 %copy-start = (bf16[1024,1024]{1,0:T(8,128)(2,1)S(1)}, bf16[1024,1024]{1,0:T(8,128)(2,1)}, u32[]{:S(2)}) copy-start(bf16[1024,1024]{1,0:T(8,128)(2,1)} %d0.5) | copy-start | bytes 6291460
  6.8 15.7 %collective-permute-start.2 = (bf16[256,1024]{1,0:T(8,128)(2,1)S(1)}, bf16[256,1024]{1,0:T(8,128)(2,1)S(1)}, u32[]{:S(2)}, u32[]{:S(2)}) collective-permute-start(bf16[256,1024]{1,0:T(8,128)(2,1)S(1)} %shard_map.29.rest), channel_id=1, source_target_pairs={{64,0},{193,1},{66,2},{195,3},{68,4},{197,5},{70,6},{199,7},{72,8}... | collective-permute-start | bytes 1572872 | tf_op jit(solution)/shard_map/ppermute | solution.py:218
  16.2 13.2 %collective-permute-start.3 = (bf16[256,1024]{1,0:T(8,128)(2,1)S(1)}, bf16[256,1024]{1,0:T(8,128)(2,1)S(1)}, u32[]{:S(2)}, u32[]{:S(2)}) collective-permute-start(bf16[256,1024]{1,0:T(8,128)(2,1)S(1)} %collective-permute-done.1.b), channel_id=1, source_target_pairs={{64,0},{451,1},{66,2},{449,3},{68,4},{455,5},{70,6},{453,7},{72,8}... | collective-permute-start | bytes 1572872 | tf_op jit(solution)/shard_map/ppermute | solution.py:223
